TPU v7x, 128 devices: a whole 4x4x4 slice. The times are simulated.
128 devices in a mesh: fsdp: 16 (over y, x), tp: 8 (over z, core).
Axes of the slice: x: 4, y: 4, z: 4, core: 2. Of those that a mesh axis runs over, the one named last changes fastest.
Arguments:
- momentum_square: float32 [2, 8192, 8192], P(None, 'fsdp', 'tp'), may hold values from -6 to 6
- grad_square: bfloat16 [2, 8192, 8192], P(None, 'fsdp', 'tp'), may hold values from -6 to 6
- basis_square: float32 [2, 8192, 256], P(None, 'tp'), may hold values from -0.0625 to 0.0625
- momentum_narrow: float32 [2, 8192, 1024], P(None, 'fsdp', 'tp'), may hold values from -6 to 6
- grad_narrow: bfloat16 [2, 8192, 1024], P(None, 'fsdp', 'tp'), may hold values from -6 to 6
- basis_narrow: float32 [2, 1024, 256], P(None, 'tp'), may hold values from -0.1875 to 0.1875
Outputs:
- new_momentum_square: float32 [2, 8192, 8192], P(None, 'fsdp', 'tp')
- new_basis_square: float32 [2, 8192, 256], P(None, 'tp')
- update_square: bfloat16 [2, 8192, 8192], P(None, 'fsdp', 'tp')
- new_momentum_narrow: float32 [2, 8192, 1024], P(None, 'fsdp', 'tp')
- new_basis_narrow: float32 [2, 1024, 256], P(None, 'tp')
- update_narrow: bfloat16 [2, 8192, 1024], P(None, 'fsdp', 'tp')
All inputs are finite; a program needn't handle non-finite values.
Results may differ from a plain program's by a relative error of at most 0.0015.
Values sent between devices are 32-bit elements; how exact they have to be, the bound alone decides.
A program may use at most 128 MiB of HBM per device.

v0:
```python
import math

import jax
import jax.numpy as jnp
from jax import lax
from jax.sharding import PartitionSpec as P

RANK = 256


MOMENTUM = 0.9


def orthonormalize(projected, gram_matrix):
    factor_lower = jnp.linalg.cholesky(gram_matrix)
    solved = jax.scipy.linalg.solve_triangular(
        factor_lower, jnp.swapaxes(projected, 1, 2), lower=True
    )
    return jnp.swapaxes(solved, 1, 2)


def gram_of(projected):
    return jnp.einsum("kmr,kms->krs", projected, projected, precision=lax.Precision.HIGHEST)


def finish(buffer, left, back, squares, fsdp_count, tp_count):
    highest = lax.Precision.HIGHEST
    new_momentum = buffer - (1.0 - MOMENTUM) * jnp.einsum(
        "kmr,knr->kmn", left, back, precision=highest
    )
    new_basis = back / (jnp.sqrt(squares) + 1e-06)[:, None, :]
    total_rows = buffer.shape[1] * fsdp_count
    total_cols = buffer.shape[2] * tp_count
    scaling = math.sqrt(total_rows * total_cols / RANK)
    update = (scaling * jnp.einsum("kmr,knr->kmn", left, new_basis, precision=highest)).astype(
        jnp.bfloat16
    )
    return (new_momentum, new_basis, update)


def local(momentum_square, grad_square, basis_square, momentum_narrow, grad_narrow, basis_narrow):
    highest = lax.Precision.HIGHEST
    fsdp_count = lax.axis_size("fsdp")
    tp_count = lax.axis_size("tp")
    buffer_square = momentum_square + grad_square.astype(jnp.float32)
    buffer_narrow = momentum_narrow + grad_narrow.astype(jnp.float32)
    projected_terms = jnp.concatenate(
        [
            jnp.einsum("kmn,knr->kmr", buffer_square, basis_square, precision=highest),
            jnp.einsum("kmn,knr->kmr", buffer_narrow, basis_narrow, precision=highest),
        ],
        axis=0,
    )
    projected = lax.psum(projected_terms, "tp")
    gram_matrix = lax.psum(gram_of(projected), "fsdp")
    left = orthonormalize(projected, gram_matrix)
    left_square = left[:2]
    left_narrow = left[2:]
    back_square = jnp.einsum("kmn,kmr->knr", buffer_square, left_square, precision=highest)
    back_narrow = jnp.einsum("kmn,kmr->knr", buffer_narrow, left_narrow, precision=highest)
    back_square, back_narrow = lax.psum((back_square, back_narrow), "fsdp")
    local_squares = jnp.concatenate(
        [jnp.sum(back_square * back_square, axis=1), jnp.sum(back_narrow * back_narrow, axis=1)],
        axis=0,
    )
    squares = lax.psum(local_squares, "tp")
    mom_square, basis_sq_new, update_sq = finish(
        buffer_square, left_square, back_square, squares[:2], fsdp_count, tp_count
    )
    mom_narrow, basis_nw_new, update_nw = finish(
        buffer_narrow, left_narrow, back_narrow, squares[2:], fsdp_count, tp_count
    )
    return (mom_square, basis_sq_new, update_sq, mom_narrow, basis_nw_new, update_nw)


def solution(mesh):
    in_specs = (
        P(None, "fsdp", "tp"),
        P(None, "fsdp", "tp"),
        P(None, "tp", None),
        P(None, "fsdp", "tp"),
        P(None, "fsdp", "tp"),
        P(None, "tp", None),
    )
    out_specs = (
        P(None, "fsdp", "tp"),
        P(None, "tp", None),
        P(None, "fsdp", "tp"),
        P(None, "fsdp", "tp"),
        P(None, "tp", None),
        P(None, "fsdp", "tp"),
    )
    return jax.shard_map(local, mesh=mesh, in_specs=in_specs, out_specs=out_specs, check_vma=False)
```

profile of v0, /device:TPU:1, one launch (start us, length us, event | category | flops | bytes accessed | tf_op | source)
XLA Modules:
  0.0 571.4 jit_solution(13125244590376869313)
XLA Ops:
  7.3 1.5 copy-done
  8.8 5.6 fusion.1
  15.4 1.5 pad_maximum_fusion
  17.0 67.3 %all-reduce.6.cloned.1.call-done = f32[4,512,256]{2,1,0:T(8,128)} async-done(((f32[4,512,256]{2,1,0:T(8,128)}), f32[4,512,256]{2,1,0:T(8,128)}) %all-reduce.6.cloned.1.call-update) | async-done | bytes 2097168 | tf_op jit(solution)/shard_map/psum | solution.py:54
  84.3 6.7 %fusion.19 = f32[4,256,256]{1,2,0:T(8,128)} fusion(f32[4,512,256]{2,1,0:T(8,128)} %all-reduce.6.cloned.1.call-done), kind=kOutput, calls=%fused_computation.53 | convolution fusion | flops 1610612736 | bytes 3145728 | tf_op jit(solution)/shard_map/kmr,kms->krs/dot_general | solution.py:23
  91.7 86.3 %all-reduce.8.cloned.1.call-done = f32[4,256,256]{1,2,0:T(8,128)} async-done(((f32[4,256,256]{1,2,0:T(8,128)}), f32[4,256,256]{1,2,0:T(8,128)}) %all-reduce.8.cloned.1.call-update) | async-done | bytes 1048592 | tf_op jit(solution)/shard_map/psum | solution.py:55
  177.9 2.6 copy.32
  180.5 1.4 fusion.9
  182.9 46.9 %custom-call.17 = f32[4,128,128]{2,1,0:T(8,128)S(1)} custom-call(f32[4,128,128]{2,1,0:T(8,128)S(1)} %cholesky.122), custom_call_target="Cholesky" | custom-call | tf_op jit(solution)/shard_map/jit(cholesky)/cholesky | solution.py:15
  229.8 39.9 %custom-call.18 = f32[4,1,128,128]{2,3,1,0:T(8,128)} custom-call(f32[4,1,128,128]{3,2,1,0:T(8,128)S(1)} %select_bitcast_fusion), custom_call_target="InvertDiagBlocksLowerTriangular" | custom-call | tf_op jit(solution)/shard_map/jit(cholesky)/cholesky | solution.py:15
  269.9 1.4 constant_dynamic-update-slice_fusion.1
  271.3 2.3 convolution_subtract_fusion.1
  273.6 48.4 %custom-call.19 = f32[4,128,128]{2,1,0:T(8,128)} custom-call(f32[4,128,128]{2,1,0:T(8,128)} %convolution_subtract_fusion.1), custom_call_target="Cholesky" | custom-call | tf_op jit(solution)/shard_map/jit(cholesky)/cholesky | solution.py:15
  322.0 1.0 select_reduce_fusion
  324.0 1.4 select_select_fusion
  325.4 5.5 while.1
  326.0 2.1 bitcast_dynamic-update-slice_fusion.2
  328.8 2.1 bitcast_dynamic-update-slice_fusion.2
  330.9 80.2 %custom-call.20 = f32[4,2,128,128]{2,3,1,0:T(8,128)} custom-call(f32[4,2,128,128]{3,2,1,0:T(8,128)} %bitcast.53), custom_call_target="InvertDiagBlocksLowerTriangular" | custom-call | tf_op jit(solution)/shard_map/jit(_solve_triangular)/vmap()/triangular_solve | solution.py:16
  411.2 2.5 fusion.7
  413.7 2.8 convolution_subtract_fusion
  416.6 1.1 fusion.11
  418.6 2.0 fusion.4
  421.1 8.0 %fusion = f32[2,1024,256]{2,1,0:T(8,128)} fusion(f32[2,512,1024]{2,1,0:T(8,128)S(1)} %copy-done.1, bf16[2,512,1024]{2,1,0:T(8,128)(2,1)S(1)} %copy-done.8, f32[4,512,256]{1,2,0:T(8,128)S(1)} %maximum_bitcast_fusion), kind=kOutput, calls=%fused_computation.8 | convolution fusion | flops 3223322624 | bytes 9437184 | tf_op jit(solution)/shard_map/kmn,kmr->knr/dot_general | solution.py:59
  429.1 91.6 %all-reduce.10.cloned.1.call-done = (f32[2,1024,256]{2,1,0:T(8,128)}, f32[2,128,256]{2,1,0:T(8,128)}) async-done(((f32[2,1024,256]{2,1,0:T(8,128)}, f32[2,128,256]{2,1,0:T(8,128)}), (f32[2,1024,256]{2,1,0:T(8,128)}, f32[2,128,256]{2,1,0:T(8,128)})) %all-reduce.10.cloned.1.call-update) | async-done | bytes 2359312 | tf_op jit(solution)/shard_map/psum | solution.py:61
  521.7 4.2 fusion.2
  525.9 1.8 multiply_reduce_fusion
  527.7 10.5 %multiply_subtract_fusion = f32[2,512,1024]{2,1,0:T(8,128)} fusion(f32[2,1024,256]{2,1,0:T(8,128)} %get-tuple-element.24, f32[2,512,1024]{2,1,0:T(8,128)S(1)} %copy-done.2, bf16[2,512,1024]{2,1,0:T(8,128)(2,1)} %param.7, f32[4,128,512]{2,1,0:T(8,128)S(1)} %copy-done.4, f32[4,128,512]{2,1,0:T(8,128)S(1)} %fusion.7), kind=kOutput, calls=%fused_computation.3 | convolution fusion | flops 3225944064 | bytes 14680064 | tf_op jit(solution)/shard_map/kmr,knr->kmn/dot_general | solution.py:28
  538.2 13.5 %psum.39 = f32[4,256]{1,0:T(4,128)S(1)} all-reduce(f32[4,256]{1,0:T(4,128)S(1)} %pad_maximum_fusion.1), channel_id=1, replica_groups=mesh['fsdp'=16,'tp'=8] {'tp'}, use_global_device_ids=true, to_apply=%region_10.11 | all-reduce | flops 1024 | bytes 8192 | tf_op jit(solution)/shard_map/psum | solution.py:66
  551.8 3.7 fusion.3
  555.7 1.0 copy-done.5
  556.7 7.9 %multiply_convert_fusion = bf16[2,512,1024]{2,1,0:T(8,128)(2,1)} fusion(f32[2,1024,256]{2,1,0:T(8,128)S(1)} %broadcast_divide_fusion, f32[4,128,512]{2,1,0:T(8,128)S(1)} %copy-done.5, f32[4,128,512]{2,1,0:T(8,128)S(1)} %fusion.7), kind=kOutput, calls=%fused_computation.2 | convolution fusion | flops 3223846912 | bytes 6291456 | tf_op jit(solution)/shard_map/kmr,knr->kmn/dot_general | solution.py:35
  (70 shorter events, 7.7 us)
Async XLA Ops:
  7.2 1.6 copy-start
  7.2 7.2 %copy-start.16 = (bf16[2,512,128]{2,1,0:T(8,128)(2,1)S(1)}, bf16[2,512,128]{2,1,0:T(8,128)(2,1)}, u32[]{:S(2)}) copy-start(bf16[2,512,128]{2,1,0:T(8,128)(2,1)} %param.10) | copy-start | bytes 786436
  7.2 7.2 %copy-start.10 = (f32[2,512,128]{2,1,0:T(8,128)S(1)}, f32[2,512,128]{2,1,0:T(8,128)}, u32[]{:S(2)}) copy-start(f32[2,512,128]{2,1,0:T(8,128)} %param.9) | copy-start | bytes 1572868
  7.2 7.2 %copy-start.21 = (f32[2,128,256]{2,1,0:T(8,128)S(1)}, f32[2,128,256]{2,1,0:T(8,128)}, u32[]{:S(2)}) copy-start(f32[2,128,256]{2,1,0:T(8,128)} %param.11) | copy-start | bytes 786436
  7.2 77.1 %all-reduce.6.cloned.1.call-start = ((), (), s32[]{:S(2)}) async-start(), calls=%async_computation | async-start | bytes 4194304 | tf_op jit(solution)/shard_map/psum | solution.py:54
  16.9 161.0 %all-reduce.8.cloned.1.call-start = ((), (), s32[]{:S(2)}) async-start(), calls=%async_computation.1 | async-start | bytes 2097152 | tf_op jit(solution)/shard_map/psum | solution.py:55
  91.0 429.7 %all-reduce.10.cloned.1.call-start = ((), (), s32[]{:S(2)}) async-start(), calls=%async_computation.2 | async-start | bytes 4718592 | tf_op jit(solution)/shard_map/psum | solution.py:61
  177.9 2.6 copy-start.12
  181.9 1.0 copy-start.14
  323.0 1.0 copy-start.13
  330.9 80.3 %copy-start.9 = (f32[4,256,256]{2,1,0:T(8,128)}, f32[4,256,256]{2,1,0:T(8,128)S(1)}, u32[]{:S(2)}) copy-start(f32[4,256,256]{2,1,0:T(8,128)S(1)} %get-tuple-element.92) | copy-start | bytes 3145732
  411.2 2.5 copy-start.6
  413.7 2.8 copy-start.20
  416.6 2.1 copy-start.11
  416.6 2.1 copy-start.17
  417.7 1.0 copy-start.3
  417.7 2.9 copy-start.1
  418.6 2.4 copy-start.8
  521.7 6.0 %copy-start.2 = (f32[2,512,1024]{2,1,0:T(8,128)S(1)}, f32[2,512,1024]{2,1,0:T(8,128)}, u32[]{:S(2)}) copy-start(f32[2,512,1024]{2,1,0:T(8,128)} %param.6) | copy-start | bytes 12582916
  521.7 6.0 %copy-start.4 = (f32[4,128,512]{2,1,0:T(8,128)S(1)}, f32[4,128,512]{2,1,0:T(8,128)}, u32[]{:S(2)}) copy-start(f32[4,128,512]{2,1,0:T(8,128)} %copy-done.3) | copy-start | bytes 3145732
  527.7 24.0 %copy-start.15 = (f32[2,128,256]{2,1,0:T(8,128)S(1)}, f32[2,128,256]{2,1,0:T(8,128)}, u32[]{:S(2)}) copy-start(f32[2,128,256]{2,1,0:T(8,128)} %get-tuple-element.25) | copy-start | bytes 786436
  551.7 3.8 copy-start.7
  551.8 3.9 copy-start.19
  555.5 1.2 copy-start.5
  556.7 7.9 %copy-start.18 = (f32[2,1024,256]{2,1,0:T(8,128)}, f32[2,1024,256]{2,1,0:T(8,128)S(1)}, u32[]{:S(2)}) copy-start(f32[2,1024,256]{2,1,0:T(8,128)S(1)} %broadcast_divide_fusion) | copy-start | bytes 6291460
Sparse Core Ops, SparseCore 0:
  17.1 67.2 all-reduce.5
  91.2 86.7 all-reduce.7
  429.2 91.3 all-reduce.9
where the time goes:
time: 578 us; the launch traced here: 571 us
  waiting for transfers between devices  245 us (42%)
  other arithmetic  224 us (39%)
  matrix products  59.8 us (10%)
  between operations  14.3 us (2%)
  local copies, waits for them, and re-layouts  13.9 us (2%)
  blocking collectives  13.5 us (2%)
    another operation x9, other arithmetic, orthonormalize(): factor_lower = jnp.linalg.cholesky(gram_matrix)  136 us
    psum x1, waiting for transfers between devices, local(): back_square, back_narrow = lax.psum((back_square, back_narrow), 'fsdp')  91.6 us
    psum x1, waiting for transfers between devices, local(): gram_matrix = lax.psum(gram_of(projected), 'fsdp')  86.3 us
    another operation x4, other arithmetic, orthonormalize(): jax.scipy.linalg.solve_triangular(factor_lower, jnp.swapaxes(projected, 1...  81.7 us
    psum x1, waiting for transfers between devices, local(): projected = lax.psum(projected_terms, 'tp')  67.3 us
    dot_general x2, matrix products, finish(): jnp.einsum('kmr,knr->kmn', left, back, precision=highest)  14.7 us
    psum x1, blocking collectives, local(): squares = lax.psum(local_squares, 'tp')  13.5 us
    dot_general x2, matrix products, finish(): jnp.einsum('kmr,knr->kmn', left, new_basis, precision=highest)  11.7 us
  transfers between devices with their start and end apart: 3, of which 3 were waited for; matrix products, arithmetic and copies ran while one was open for 0% of the time, Pallas kernels for 0%

commit v1 on v0

v1 whole, which is shorter than its diff:
```python
import math

import jax
import jax.numpy as jnp
from jax import lax
from jax.experimental import pallas as pl
from jax.experimental.pallas import tpu as pltpu
from jax.sharding import PartitionSpec as P

RANK = 256
MOMENTUM = 0.9
MESH = pl.DeviceIdType.MESH
F32 = jnp.float32
BF16 = jnp.bfloat16
PANEL = 32
GROUP = 8
VMEM_LIMIT = 56 * 2**20

RING_X, RING_Y, RING_Z = 4, 4, 4


def split(x):
    hi = x.astype(BF16)
    return hi, (x - hi.astype(F32)).astype(BF16)


def mm(a, b, dims=((1,), (0,))):
    return lax.dot_general(a, b, (dims, ((), ())), preferred_element_type=F32)


def dot3(a, b, dims=((1,), (0,))):
    return mm(a[0], b[0], dims) + (mm(a[0], b[1], dims) + mm(a[1], b[0], dims))


def dot6(a, b, dims=((1,), (0,))):
    return lax.dot_general(
        a, b, (dims, ((), ())), precision=lax.Precision.HIGHEST, preferred_element_type=F32
    )


class Links:
    def __init__(self, send, recv):
        self.send, self.recv, self.used = send, recv, 0

    def take(self, count):
        self.used += count
        return self.used - count

    def copy(self, index, src, dst, device):
        return pltpu.make_async_remote_copy(
            src_ref=src,
            dst_ref=dst,
            send_sem=self.send.at[index],
            recv_sem=self.recv.at[index],
            device_id=device,
            device_id_type=MESH,
        )


class Scatter:
    def __init__(self, links, me, right, left, part, half, inbox):
        self.me, self.part, self.half, self.inbox = me, part, half, inbox
        self.after, self.before = lax.rem(me + 1, 4), lax.rem(me + 3, 4)
        opposite = lax.rem(me + 2, 4)
        base = links.take(6)

        def outgoing(slot, view, device):
            return links.copy(base + slot, view, inbox.at[slot], device)

        h = half
        self.r1 = outgoing(0, part(opposite, 0, h), right)
        self.r2 = outgoing(1, part(self.after, h, h), right)
        self.r3 = outgoing(2, part(self.after, 0, h), right)
        self.l1 = outgoing(3, part(opposite, h, h), left)
        self.l2 = outgoing(4, part(self.before, 0, h), left)
        self.l3 = outgoing(5, part(self.before, h, h), left)

    def start(self):
        for c in (self.r1, self.l1, self.r2, self.l2):
            c.start()

    def middle(self):
        h = self.half
        self.r1.wait_recv()
        view = self.part(self.after, 0, h)
        view[...] = view[...] + self.inbox[0]
        self.r3.start()
        self.l1.wait_recv()
        view = self.part(self.before, h, h)
        view[...] = view[...] + self.inbox[3]
        self.l3.start()

    def end(self, target):
        h = self.half
        self.r2.wait_recv()
        self.l2.wait_recv()
        self.r3.wait_recv()
        target(0, h)[...] = self.part(self.me, 0, h)[...] + (self.inbox[2] + self.inbox[4])
        self.l3.wait_recv()
        target(h, h)[...] = self.part(self.me, h, h)[...] + (self.inbox[1] + self.inbox[5])

    def drain(self):
        for c in (self.r1, self.r2, self.r3, self.l1, self.l2, self.l3):
            c.wait_send()


class Gather:
    def __init__(self, links, me, right, left, part, half):
        after, before = lax.rem(me + 1, 4), lax.rem(me + 3, 4)
        base = links.take(4)
        h = half

        def outgoing(slot, view, device):
            return links.copy(base + slot, view, view, device)

        self.r1 = outgoing(0, part(me, 0, 2 * h), right)
        self.l1 = outgoing(1, part(me, 0, 2 * h), left)
        self.r2 = outgoing(2, part(before, 0, h), right)
        self.l2 = outgoing(3, part(after, h, h), left)

    def start(self):
        self.r1.start()
        self.l1.start()

    def middle(self):
        self.r1.wait_recv()
        self.r2.start()
        self.l1.wait_recv()
        self.l2.start()

    def end(self):
        self.r2.wait_recv()
        self.l2.wait_recv()

    def drain(self):
        for c in (self.r1, self.l1, self.r2, self.l2):
            c.wait_send()


def factor_block(a):
    rows = lax.broadcasted_iota(jnp.int32, (PANEL, 128), 0)
    done = []
    for s in range(0, PANEL, GROUP):
        n = PANEL - s
        cols = [jnp.broadcast_to(a[s:, s + j : s + j + 1], (n, 128)) for j in range(GROUP)]
        lines = [a[s + j : s + j + 1, :] for j in range(GROUP)]
        rest = a[s + GROUP :]
        for j in range(GROUP):
            pivot = cols[j][j : j + 1, :]
            m = jnp.where(rows[s:] > s + j, cols[j] * (1.0 / pivot), 0.0)
            for q in range(j + 1, GROUP):
                cols[q] = cols[q] - m * cols[q][j : j + 1, :]
            for q in range(j + 1, GROUP):
                lines[q] = lines[q] - m[q : q + 1, :] * lines[j]
            if n > GROUP:
                rest = rest - m[GROUP:] * lines[j]
            done.append(lines[j] * lax.rsqrt(pivot))
        if n > GROUP:
            a = jnp.concatenate([a[: s + GROUP], rest], axis=0)
    return jnp.concatenate(done, axis=0)


def cholesky_start(gram, work):
    n = RANK
    work[:, :n] = gram[...]
    eye = lax.broadcasted_iota(jnp.int32, (n, n), 0) == lax.broadcasted_iota(jnp.int32, (n, n), 1)
    work[:, n:] = eye.astype(F32)


def cholesky_panels(work, inverse, first, last):
    n = RANK
    lane = lax.broadcasted_iota(jnp.int32, (PANEL, 128), 1)
    row = lax.broadcasted_iota(jnp.int32, (PANEL, 128), 0)

    def panel(k, carry):
        off = pl.multiple_of(k * PANEL, PANEL)
        band = work[pl.ds(off, PANEL), :]
        block = pltpu.roll(band[:, :n], lax.rem(n - off, n), axis=1)[:, :128]
        both = jnp.where(lane < PANEL, block, jnp.where(lane == row + PANEL, 1.0, 0.0))
        block_inverse = factor_block(both)[:, PANEL : 2 * PANEL]
        band = dot6(block_inverse, band)
        inverse[pl.ds(off, PANEL), :] = band[:, n:]
        work[...] = work[...] - dot6(band[:, :n], band, ((0,), (0,)))
        return carry

    lax.fori_loop(first, last, panel, 0)


def orthonormal_kernel(
    mom_sq, grad_sq, basis_sq, mom_nw, grad_nw, basis_nw,
    left_out, back_out, squares_out,
    mom_sq_v, grad_sq_v, basis_sq_v, mom_nw_v, grad_nw_v, basis_nw_v,
    buf_sq_hi, buf_sq_lo, buf_nw_hi, buf_nw_lo,
    partial, held, projected, scatter_z,
    gram_part, gram_in, gram, chol_work, inverse,
    sums, wide, scatter_1, scatter_2,
    norms,
    load_sem, send_sem, recv_sem, gram_send, gram_recv, gram_send2, gram_recv2, norm_send, norm_recv,
):
    f, t = lax.axis_index("fsdp"), lax.axis_index("tp")
    y, x = f // RING_X, lax.rem(f, RING_X)
    z, core = t // 2, lax.rem(t, 2)
    other = 1 - core
    fsdp_count = RING_X * RING_Y
    tp_count = RING_Z * 2
    links = Links(send_sem, recv_sem)

    def at(y=y, x=x, z=z, core=core):
        return (y * RING_X + x, z * 2 + core)

    def step(value, by):
        return lax.rem(value + by, 4)

    sibling = at(core=other)
    x_right, x_left = at(x=step(x, 1)), at(x=step(x, 3))
    y_right, y_left = at(y=step(y, 1)), at(y=step(y, 3))
    z_right, z_left = at(z=step(z, 1)), at(z=step(z, 3))

    barrier = pltpu.get_barrier_semaphore()

    def greet_fsdp(k, carry):
        peer = lax.rem(f + k, fsdp_count)
        pl.semaphore_signal(barrier, inc=1, device_id=(peer, t), device_id_type=MESH)
        return carry

    def greet_tp(k, carry):
        peer = lax.rem(t + k, tp_count)
        pl.semaphore_signal(barrier, inc=1, device_id=(f, peer), device_id_type=MESH)
        return carry

    lax.fori_loop(1, fsdp_count, greet_fsdp, 0)
    lax.fori_loop(1, tp_count, greet_tp, 0)

    loads = []
    for k in range(2):
        for n, (src, dst) in enumerate(
            ((basis_sq, basis_sq_v), (mom_sq, mom_sq_v), (grad_sq, grad_sq_v))
        ):
            loads.append(pltpu.make_async_copy(src.at[k], dst.at[k], load_sem.at[k * 3 + n]))
    for n, (src, dst) in enumerate(
        ((basis_nw, basis_nw_v), (mom_nw, mom_nw_v), (grad_nw, grad_nw_v))
    ):
        loads.append(pltpu.make_async_copy(src, dst, load_sem.at[6 + n]))
    for c in loads:
        c.start()

    def rows_of(which):
        return pl.ds(pl.multiple_of(which * 256, 256), 256)

    core_base = links.take(4)
    core_copies = [
        links.copy(core_base + i, partial.at[i, rows_of(other)], held.at[i], sibling)
        for i in range(4)
    ]

    def project(i, mom, grad, basis, hi, lo):
        pair = split(basis[...])
        for place, which in enumerate((other, core)):
            rows = rows_of(which)
            b_hi, b_lo = split(mom[rows, :] + grad[rows, :].astype(F32))
            hi[rows, :] = b_hi
            lo[rows, :] = b_lo
            partial[i, rows, :] = dot3((b_hi, b_lo), pair)
            if place == 0:
                if i == 0:
                    pl.semaphore_wait(barrier, fsdp_count + tp_count - 2)
                core_copies[i].start()

    for k in range(2):
        for c in loads[k * 3 : k * 3 + 3]:
            c.wait()
        project(
            k, mom_sq_v.at[k], grad_sq_v.at[k], basis_sq_v.at[k], buf_sq_hi.at[k], buf_sq_lo.at[k]
        )
    for c in loads[6:]:
        c.wait()
    for k in range(2):
        project(
            2 + k, mom_nw_v.at[k], grad_nw_v.at[k], basis_nw_v.at[k], buf_nw_hi.at[k], buf_nw_lo.at[k]
        )
    for i in range(4):
        core_copies[i].wait_recv()
        held[i] = held[i] + partial[i, rows_of(core), :]

    z_sum = Scatter(
        links, z, z_right, z_left, lambda i, a, n: held.at[i, pl.ds(a, n)], 128, scatter_z
    )

    def own_rows(i, a, n):
        return projected.at[i, pl.ds(pl.multiple_of(core * 256 + a, 128), n)]

    z_all = Gather(links, z, z_right, z_left, own_rows, 128)
    z_sum.start()
    z_sum.middle()
    z_sum.end(lambda a, n: own_rows(z, a, n))
    z_all.start()

    core_base = links.take(4)

    def core_send(n, i):
        view = own_rows(i, 0, 256)
        return links.copy(core_base + n, view, view, sibling)

    across = [core_send(n, step(z, by)) for n, by in enumerate((0, 3, 1, 2))]
    across[0].start()

    across[0].wait_recv()
    gram_cols = pl.ds(pl.multiple_of(core * 128, 128), 128)
    gram_part[...] = dot6(projected[z, :, gram_cols], projected[z], ((0,), (0,)))

    def gram_rows(i):
        return pl.ds(pl.multiple_of(i * 8, 8), 8)

    def gram_copy(peer, slot):
        return pltpu.make_async_remote_copy(
            src_ref=gram_part.at[gram_rows(peer)],
            dst_ref=gram_in.at[slot],
            send_sem=gram_send.at[peer],
            recv_sem=gram_recv.at[slot],
            device_id=(peer, t),
            device_id_type=MESH,
        )

    def gram_out(k, carry):
        gram_copy(lax.rem(f + k, fsdp_count), f).start()
        return carry

    lax.fori_loop(1, fsdp_count, gram_out, 0)
    gram_in[f] = gram_part[gram_rows(f), :]

    z_all.middle()
    across[1].start()
    across[2].start()

    def gram_arrive(k, carry):
        gram_copy(lax.rem(f + k, fsdp_count), lax.rem(f + k, fsdp_count)).wait_recv()
        return carry

    lax.fori_loop(1, fsdp_count, gram_arrive, 0)

    def full_rows(i):
        return pl.ds(pl.multiple_of(core * 128 + i * 8, 8), 8)

    gram[full_rows(f), :] = jnp.sum(gram_in[...], axis=0)

    def gram_copy2(peer, slot):
        view = gram.at[full_rows(slot)]
        return pltpu.make_async_remote_copy(
            src_ref=view,
            dst_ref=view,
            send_sem=gram_send2.at[peer],
            recv_sem=gram_recv2.at[slot],
            device_id=(peer, t),
            device_id_type=MESH,
        )

    def gram_out2(k, carry):
        gram_copy2(lax.rem(f + k, fsdp_count), f).start()
        return carry

    lax.fori_loop(1, fsdp_count, gram_out2, 0)

    z_all.end()
    across[3].start()
    for c in across[1:]:
        c.wait_recv()

    def back_product(k):
        sq = split(projected[k].T)
        sums[k, :, :1024] = dot3(sq, (buf_sq_hi[k], buf_sq_lo[k]))
        nw = split(projected[2 + k].T)
        sums[k, :, 1024:] = dot3(nw, (buf_nw_hi[k], buf_nw_lo[k]))

    def wide_rows(ref, k):
        return lambda i, a, n: ref.at[k, pl.ds(pl.multiple_of(i * 64 + a, 8), n)]

    def narrow_rows(ref, k, outer):
        return lambda i, a, n: ref.at[k, pl.ds(pl.multiple_of(outer * 64 + i * 16 + a, 8), n)]

    sum_1 = [
        Scatter(links, x, x_right, x_left, wide_rows(sums, 0), 32, scatter_1.at[0]),
        Scatter(links, y, y_right, y_left, wide_rows(sums, 1), 32, scatter_1.at[1]),
    ]
    sum_2 = [
        Scatter(links, y, y_right, y_left, narrow_rows(sums, 0, x), 8, scatter_2.at[0]),
        Scatter(links, x, x_right, x_left, narrow_rows(sums, 1, y), 8, scatter_2.at[1]),
    ]
    all_1 = [
        Gather(links, y, y_right, y_left, narrow_rows(wide, 0, x), 8),
        Gather(links, x, x_right, x_left, narrow_rows(wide, 1, y), 8),
    ]
    all_2 = [
        Gather(links, x, x_right, x_left, wide_rows(wide, 0), 32),
        Gather(links, y, y_right, y_left, wide_rows(wide, 1), 32),
    ]
    outer, inner = (x, y), (y, x)

    back_product(0)
    sum_1[0].start()
    back_product(1)
    sum_1[1].start()

    def gram_arrive2(k, carry):
        gram_copy2(lax.rem(f + k, fsdp_count), lax.rem(f + k, fsdp_count)).wait_recv()
        return carry

    lax.fori_loop(1, fsdp_count, gram_arrive2, 0)
    half_rows = gram.at[pl.ds(pl.multiple_of(core * 128, 128), 128)]
    gram_across = links.copy(links.take(1), half_rows, half_rows, sibling)
    gram_across.start()
    gram_across.wait_recv()

    own_inverse = inverse.at[z]
    cholesky_start(gram, chol_work)
    cholesky_panels(chol_work, own_inverse, 0, 1)
    for k in range(2):
        sum_1[k].middle()
    cholesky_panels(chol_work, own_inverse, 1, 3)
    for k in range(2):
        sum_1[k].end(lambda a, n, k=k: wide_rows(sums, k)(outer[k], a, n))
        sum_2[k].start()
    cholesky_panels(chol_work, own_inverse, 3, 4)
    for k in range(2):
        sum_2[k].middle()
    cholesky_panels(chol_work, own_inverse, 4, 5)
    for k in range(2):
        sum_2[k].end(lambda a, n, k=k: narrow_rows(wide, k, outer[k])(inner[k], a, n))
        all_1[k].start()
    cholesky_panels(chol_work, own_inverse, 5, 6)
    for k in range(2):
        all_1[k].middle()
    cholesky_panels(chol_work, own_inverse, 6, 7)
    for k in range(2):
        all_1[k].end()
        all_2[k].start()
    cholesky_panels(chol_work, own_inverse, 7, 8)

    def inverse_rows(i, a, n):
        return inverse.at[i, pl.ds(pl.multiple_of(core * 128 + a, 64), n)]

    inv_all = Gather(links, z, z_right, z_left, inverse_rows, 64)
    inv_all.start()
    core_base = links.take(3)

    def inverse_send(n, i):
        view = inverse_rows(i, 0, 128)
        return links.copy(core_base + n, view, view, sibling)

    inv_across = [inverse_send(n, step(z, by)) for n, by in enumerate((3, 1, 2))]
    inv_all.middle()
    inv_across[0].start()
    inv_across[1].start()
    for k in range(2):
        all_2[k].middle()
    inv_all.end()
    inv_across[2].start()
    for c in inv_across:
        c.wait_recv()

    for i in range(4):
        left_out[i] = dot3(split(projected[i]), split(inverse[i]), ((1,), (1,)))

    norms[t] = jnp.zeros((8, RANK), F32)
    for k in range(2):
        all_2[k].end()
        for i, cols in ((k, slice(0, 1024)), (2 + k, slice(1024, 1152))):
            back = dot3(split(inverse[i]), split(wide[k, :, cols]))
            back_out[k, :, cols] = back
            square = dot6(jnp.ones((8, back.shape[1]), F32), back * back, ((1,), (1,)))
            norms[t, pl.ds(i, 1), :] = square[:1]

    def norm_copy(peer, slot):
        return pltpu.make_async_remote_copy(
            src_ref=norms.at[t],
            dst_ref=norms.at[slot],
            send_sem=norm_send.at[peer],
            recv_sem=norm_recv.at[slot],
            device_id=(f, peer),
            device_id_type=MESH,
        )

    def norm_out(k, carry):
        norm_copy(lax.rem(t + k, tp_count), t).start()
        return carry

    def norm_arrive(k, carry):
        norm_copy(lax.rem(t + k, tp_count), lax.rem(t + k, tp_count)).wait_recv()
        return carry

    lax.fori_loop(1, tp_count, norm_out, 0)
    lax.fori_loop(1, tp_count, norm_arrive, 0)
    squares_out[...] = jnp.sum(norms[...], axis=0)

    for c in core_copies + across + inv_across + [gram_across]:
        c.wait_send()
    for ring in [z_sum, z_all, inv_all] + sum_1 + sum_2 + all_1 + all_2:
        ring.drain()

    def gram_drain(k, carry):
        peer = lax.rem(f + k, fsdp_count)
        gram_copy(peer, f).wait_send()
        gram_copy2(peer, f).wait_send()
        return carry

    def norm_drain(k, carry):
        norm_copy(lax.rem(t + k, tp_count), t).wait_send()
        return carry

    lax.fori_loop(1, fsdp_count, gram_drain, 0)
    lax.fori_loop(1, tp_count, norm_drain, 0)


def orthonormal(mom_sq, grad_sq, basis_sq, mom_nw, grad_nw, basis_nw):
    rows = mom_sq.shape[1]
    wide, thin = mom_sq.shape[2], mom_nw.shape[2]
    both = wide + thin
    vmem = pltpu.VMEM
    dma = pltpu.SemaphoreType.DMA
    whole = pl.BlockSpec(memory_space=pltpu.VMEM)
    return pl.pallas_call(
        orthonormal_kernel,
        out_shape=(
            jax.ShapeDtypeStruct((4, rows, RANK), F32),
            jax.ShapeDtypeStruct((2, RANK, both), F32),
            jax.ShapeDtypeStruct((8, RANK), F32),
        ),
        in_specs=[pl.BlockSpec(memory_space=pl.ANY)] * 6,
        out_specs=(whole, whole, whole),
        scratch_shapes=[
            vmem(mom_sq.shape, F32),
            vmem(grad_sq.shape, BF16),
            vmem(basis_sq.shape, F32),
            vmem(mom_nw.shape, F32),
            vmem(grad_nw.shape, BF16),
            vmem(basis_nw.shape, F32),
            vmem(mom_sq.shape, BF16),
            vmem(mom_sq.shape, BF16),
            vmem(mom_nw.shape, BF16),
            vmem(mom_nw.shape, BF16),
            vmem((4, rows, RANK), F32),
            vmem((4, rows // 2, RANK), F32),
            vmem((4, rows, RANK), F32),
            vmem((6, rows // 4, RANK), F32),
            vmem((128, RANK), F32),
            vmem((16, 8, RANK), F32),
            vmem((RANK, RANK), F32),
            vmem((RANK, 2 * RANK), F32),
            vmem((4, RANK, RANK), F32),
            vmem((2, RANK, both), F32),
            vmem((2, RANK, both), F32),
            vmem((2, 6, 32, both), F32),
            vmem((2, 6, 8, both), F32),
            vmem((8, 8, RANK), F32),
            dma((9,)),
            dma((72,)),
            dma((72,)),
            dma((16,)),
            dma((16,)),
            dma((16,)),
            dma((16,)),
            dma((8,)),
            dma((8,)),
        ],
        compiler_params=pltpu.CompilerParams(
            collective_id=0, has_side_effects=True, vmem_limit_bytes=VMEM_LIMIT
        ),
        cost_estimate=pl.CostEstimate(flops=6 * 10**9, bytes_accessed=14 * 2**20, transcendentals=0),
        name="orthonormal",
    )(mom_sq, grad_sq, basis_sq, mom_nw, grad_nw, basis_nw)


def finish_kernel(
    scale_sq, scale_nw,
    mom_sq, grad_sq, mom_nw, grad_nw, left_sq, left_nw, back, squares,
    mom_sq_out, basis_sq_out, upd_sq_out, mom_nw_out, basis_nw_out, upd_nw_out,
    back_hi, back_lo,
):
    k, i = pl.program_id(0), pl.program_id(1)
    wide = mom_sq.shape[2]

    @pl.when(i == 0)
    def _():
        back_hi[...], back_lo[...] = split(back[0])

    def part(which, mom, grad, left, cols, scale, mom_out, upd_out):
        divisor = jnp.sqrt(squares[pl.ds(which, 1), :]) + 1e-06
        pair = (back_hi[:, cols], back_lo[:, cols])
        mom_out[0] = (mom[0] + grad[0].astype(F32)) - (1.0 - MOMENTUM) * dot3(split(left[0]), pair)
        upd_out[0] = (scale * dot3(split(left[0] / divisor), pair)).astype(BF16)
        return divisor

    divisor_sq = part(k, mom_sq, grad_sq, left_sq, slice(0, wide), scale_sq, mom_sq_out, upd_sq_out)
    divisor_nw = part(
        2 + k, mom_nw, grad_nw, left_nw, slice(wide, None), scale_nw, mom_nw_out, upd_nw_out
    )
    n = basis_sq_out.shape[1]
    cols = pl.ds(pl.multiple_of(i * n, n), n)
    basis_sq_out[0] = back[0, :, cols].T / divisor_sq

    @pl.when(i == 0)
    def _():
        basis_nw_out[0] = back[0, :, wide:].T / divisor_nw


def finish(mom_sq, grad_sq, mom_nw, grad_nw, left, back, squares, scale_sq, scale_nw):
    pairs, rows, wide = mom_sq.shape
    thin = mom_nw.shape[2]
    steps = 4
    block = rows // steps

    def by_rows(width, first=0):
        return pl.BlockSpec((1, block, width), lambda k, i: (first + k, i, 0))

    def kernel(*refs):
        finish_kernel(scale_sq, scale_nw, *refs)

    return pl.pallas_call(
        kernel,
        grid=(pairs, steps),
        in_specs=[
            by_rows(wide),
            by_rows(wide),
            by_rows(thin),
            by_rows(thin),
            by_rows(RANK),
            by_rows(RANK, 2),
            pl.BlockSpec((1, RANK, wide + thin), lambda k, i: (k, 0, 0)),
            pl.BlockSpec((8, RANK), lambda k, i: (0, 0)),
        ],
        out_specs=(
            by_rows(wide),
            pl.BlockSpec((1, wide // steps, RANK), lambda k, i: (k, i, 0)),
            by_rows(wide),
            by_rows(thin),
            pl.BlockSpec((1, thin, RANK), lambda k, i: (k, 0, 0)),
            by_rows(thin),
        ),
        out_shape=(
            jax.ShapeDtypeStruct(mom_sq.shape, F32),
            jax.ShapeDtypeStruct((pairs, wide, RANK), F32),
            jax.ShapeDtypeStruct(mom_sq.shape, BF16),
            jax.ShapeDtypeStruct(mom_nw.shape, F32),
            jax.ShapeDtypeStruct((pairs, thin, RANK), F32),
            jax.ShapeDtypeStruct(mom_nw.shape, BF16),
        ),
        scratch_shapes=[
            pltpu.VMEM((RANK, wide + thin), BF16),
            pltpu.VMEM((RANK, wide + thin), BF16),
        ],
        compiler_params=pltpu.CompilerParams(vmem_limit_bytes=VMEM_LIMIT),
        cost_estimate=pl.CostEstimate(flops=4 * 10**9, bytes_accessed=18 * 2**20, transcendentals=0),
        name="finish",
    )(mom_sq, grad_sq, mom_nw, grad_nw, left, left, back, squares)


def local(momentum_square, grad_square, basis_square, momentum_narrow, grad_narrow, basis_narrow):
    left, back, squares = orthonormal(
        momentum_square, grad_square, basis_square, momentum_narrow, grad_narrow, basis_narrow
    )
    total_rows = momentum_square.shape[1] * lax.axis_size("fsdp")
    tp_count = lax.axis_size("tp")
    scale_sq = math.sqrt(total_rows * momentum_square.shape[2] * tp_count / RANK)
    scale_nw = math.sqrt(total_rows * momentum_narrow.shape[2] * tp_count / RANK)
    return finish(
        momentum_square, grad_square, momentum_narrow, grad_narrow, left, back, squares, scale_sq, scale_nw
    )


def solution(mesh):
    by_both = P(None, "fsdp", "tp")
    by_tp = P(None, "tp", None)
    return jax.shard_map(
        local,
        mesh=mesh,
        in_specs=(by_both, by_both, by_tp, by_both, by_both, by_tp),
        out_specs=(by_both, by_tp, by_both, by_both, by_tp, by_both),
        check_vma=False,
    )
```

time: 578 us -> 106 us (0.18); the launches traced: 571 us -> 105 us
  waiting for transfers between devices: 245 us -> 0 us
  other arithmetic: 224 us -> 0 us
  Pallas kernels: 0 us -> 105 us
  matrix products: 59.8 us -> 0 us
  local copies, waits for them, and re-layouts: 13.9 us -> 0 us
  blocking collectives: 13.5 us -> 0 us
  between operations: 14.3 us -> 0.8 us
    psum x3 -> x0, waiting for transfers between devices: 245 us -> none  [the longest x1 91.6 us: local(): back_square, back_narrow = lax.psum((back_square, back_narrow), 'fsdp')]
    another operation x13 -> x0, other arithmetic: 218 us -> none  [the longest x9 136 us: orthonormalize(): factor_lower = jnp.linalg.cholesky(gram_matrix)]
    pallas_call x0 -> x2, Pallas kernels: none -> 105 us  [the longest x1 91.9 us: orthonormal(): pl.pallas_call(orthonormal_kernel, out_shape=(jax.ShapeDtypeStruct((4, ro...]
    dot_general x9 -> x0, matrix products: 49.7 us -> none  [the longest x2 14.7 us: finish(): jnp.einsum('kmr,knr->kmn', left, back, precision=highest)]
    psum x1 -> x0, blocking collectives: 13.5 us -> none  [local(): squares = lax.psum(local_squares, 'tp')]
    another operation x5 -> x0, matrix products: 10.1 us -> none  [the longest x3 6.39 us: orthonormalize(): jax.scipy.linalg.solve_triangular(factor_lower, jnp.swapaxes(projected, 1...]
  transfers between devices with their start and end apart: 3 -> 0, of which waited for: 3 -> 0; matrix products, arithmetic and copies ran while one was open for 0% -> 0% of each run, Pallas kernels for 0% -> 0%
where the time goes in v1:
time: 106 us; the launch traced here: 105 us
  Pallas kernels  105 us (99%)
    pallas_call x1, Pallas kernels, orthonormal(): pl.pallas_call(orthonormal_kernel, out_shape=(jax.ShapeDtypeStruct((4, ro...  91.9 us
    pallas_call x1, Pallas kernels, finish(): pl.pallas_call(kernel, grid=(pairs, steps), in_specs=[by_rows(wide), by_r...  12.8 us

profile of v1, /device:TPU:1, one launch (start us, length us, event | category | flops | bytes accessed | tf_op | source)
XLA Modules:
  0.0 105.4 jit_solution(12847772799157578212)
XLA Ops:
  0.6 91.9 %orthonormal.1 = (f32[4,512,256]{2,1,0:T(8,128)}, f32[2,256,1152]{2,1,0:T(8,128)}, f32[8,256]{1,0:T(8,128)}) custom-call(f32[2,512,1024]{2,1,0:T(8,128)} %refs_0_.1, bf16[2,512,1024]{2,1,0:T(8,128)(2,1)} %refs_1_.1, f32[2,1024,256]{2,1,0:T(8,128)} %basis_sq.1, f32[2,512,128]{2,1,0:T(8,128)} %refs_2_.1, bf16[2,512,128]{2,1,0:T(8,128)(2,1)} %refs_3_.1, ...), custom_call_target="tpu_custom_call" | custom-call | flops 6000000000 | bytes 14680064 | tf_op jit(solution)/shard_map/orthonormal/pallas_call | solution.py:520
  92.5 12.8 %finish.1 = (f32[2,512,1024]{2,1,0:T(8,128)}, f32[2,1024,256]{2,1,0:T(8,128)}, bf16[2,512,1024]{2,1,0:T(8,128)(2,1)}, f32[2,512,128]{2,1,0:T(8,128)}, f32[2,128,...) custom-call(f32[2,512,1024]{2,1,0:T(8,128)} %refs_0_.1, bf16[2,512,1024]{2,1,0:T(8,128)(2,1)} %refs_1_.1, ...), custom_call_target="tpu_custom_call" | custom-call | flops 4000000000 | bytes 18874368 | tf_op jit(solution)/shard_map/finish/pallas_call | solution.py:617

commit v2 on v1

v2 whole, which is shorter than its diff:
```python
import math

import jax
import jax.numpy as jnp
from jax import lax
from jax.experimental import pallas as pl
from jax.experimental.pallas import tpu as pltpu
from jax.sharding import PartitionSpec as P

RANK = 256
MOMENTUM = 0.9
MESH = pl.DeviceIdType.MESH
F32 = jnp.float32
BF16 = jnp.bfloat16
PANEL = 32
GROUP = 8
VMEM_LIMIT = 40 * 2**20

RING_X, RING_Y, RING_Z = 4, 4, 4


def split(x):
    hi = x.astype(BF16)
    return hi, (x - hi.astype(F32)).astype(BF16)


def mm(a, b, dims=((1,), (0,))):
    return lax.dot_general(a, b, (dims, ((), ())), preferred_element_type=F32)


def dot3(a, b, dims=((1,), (0,))):
    return mm(a[0], b[0], dims) + (mm(a[0], b[1], dims) + mm(a[1], b[0], dims))


def dot6(a, b, dims=((1,), (0,))):
    return lax.dot_general(
        a, b, (dims, ((), ())), precision=lax.Precision.HIGHEST, preferred_element_type=F32
    )


class Links:
    def __init__(self, send, recv):
        self.send, self.recv, self.sent, self.received = send, recv, 0, 0

    def group(self, ruler):
        return Group(self, ruler)


class Group:
    def __init__(self, links, ruler):
        self.links, self.ruler = links, ruler
        self.sem = links.send.at[links.sent]
        links.sent += 1

    def copy(self, src, dst, device):
        index = self.links.received
        self.links.received += 1
        return pltpu.make_async_remote_copy(
            src_ref=src,
            dst_ref=dst,
            send_sem=self.sem,
            recv_sem=self.links.recv.at[index],
            device_id=device,
            device_id_type=MESH,
        )

    def drain(self):
        pltpu.make_async_copy(self.ruler, self.ruler, self.sem).wait()


class Scatter:
    def __init__(self, links, me, right, left, part, half, inbox):
        self.me, self.part, self.half, self.inbox = me, part, half, inbox
        self.after, self.before = lax.rem(me + 1, 4), lax.rem(me + 3, 4)
        opposite = lax.rem(me + 2, 4)
        self.group = links.group(inbox)

        def outgoing(slot, view, device):
            return self.group.copy(view, inbox.at[slot], device)

        h = half
        self.r1 = outgoing(0, part(opposite, 0, h), right)
        self.r2 = outgoing(1, part(self.after, h, h), right)
        self.r3 = outgoing(2, part(self.after, 0, h), right)
        self.l1 = outgoing(3, part(opposite, h, h), left)
        self.l2 = outgoing(4, part(self.before, 0, h), left)
        self.l3 = outgoing(5, part(self.before, h, h), left)

    def start(self):
        for c in (self.r1, self.l1, self.r2, self.l2):
            c.start()

    def middle(self):
        h = self.half
        self.r1.wait_recv()
        view = self.part(self.after, 0, h)
        view[...] = view[...] + self.inbox[0]
        self.r3.start()
        self.l1.wait_recv()
        view = self.part(self.before, h, h)
        view[...] = view[...] + self.inbox[3]
        self.l3.start()

    def end(self, target):
        h = self.half
        self.r2.wait_recv()
        self.l2.wait_recv()
        self.r3.wait_recv()
        target(0, h)[...] = self.part(self.me, 0, h)[...] + (self.inbox[2] + self.inbox[4])
        self.l3.wait_recv()
        target(h, h)[...] = self.part(self.me, h, h)[...] + (self.inbox[1] + self.inbox[5])


class Gather:
    def __init__(self, links, me, right, left, part, half, ruler):
        after, before = lax.rem(me + 1, 4), lax.rem(me + 3, 4)
        self.group = links.group(ruler)
        h = half

        def outgoing(view, device):
            return self.group.copy(view, view, device)

        self.r1 = outgoing(part(me, 0, 2 * h), right)
        self.l1 = outgoing(part(me, 0, 2 * h), left)
        self.r2 = outgoing(part(before, 0, h), right)
        self.l2 = outgoing(part(after, h, h), left)

    def start(self):
        self.r1.start()
        self.l1.start()

    def middle(self):
        self.r1.wait_recv()
        self.r2.start()
        self.l1.wait_recv()
        self.l2.start()

    def end(self):
        self.r2.wait_recv()
        self.l2.wait_recv()


def factor_block(a):
    rows = lax.broadcasted_iota(jnp.int32, (PANEL, 128), 0)
    done = []
    for s in range(0, PANEL, GROUP):
        n = PANEL - s
        cols = [jnp.broadcast_to(a[s:, s + j : s + j + 1], (n, 128)) for j in range(GROUP)]
        lines = [a[s + j : s + j + 1, :] for j in range(GROUP)]
        rest = a[s + GROUP :]
        for j in range(GROUP):
            pivot = cols[j][j : j + 1, :]
            m = jnp.where(rows[s:] > s + j, cols[j] * (1.0 / pivot), 0.0)
            for q in range(j + 1, GROUP):
                cols[q] = cols[q] - m * cols[q][j : j + 1, :]
            for q in range(j + 1, GROUP):
                lines[q] = lines[q] - m[q : q + 1, :] * lines[j]
            if n > GROUP:
                rest = rest - m[GROUP:] * lines[j]
            done.append(lines[j] * lax.rsqrt(pivot))
        if n > GROUP:
            a = jnp.concatenate([a[: s + GROUP], rest], axis=0)
    return jnp.concatenate(done, axis=0)


def cholesky_start(gram, work):
    n = RANK
    work[:, :n] = gram[...]
    eye = lax.broadcasted_iota(jnp.int32, (n, n), 0) == lax.broadcasted_iota(jnp.int32, (n, n), 1)
    work[:, n:] = eye.astype(F32)


def cholesky_panels(work, inverse, first, last):
    n = RANK
    lane = lax.broadcasted_iota(jnp.int32, (PANEL, 128), 1)
    row = lax.broadcasted_iota(jnp.int32, (PANEL, 128), 0)

    def panel(k, carry):
        off = pl.multiple_of(k * PANEL, PANEL)
        band = work[pl.ds(off, PANEL), :]
        block = pltpu.roll(band[:, :n], lax.rem(n - off, n), axis=1)[:, :128]
        both = jnp.where(lane < PANEL, block, jnp.where(lane == row + PANEL, 1.0, 0.0))
        block_inverse = factor_block(both)[:, PANEL : 2 * PANEL]
        band = dot6(block_inverse, band)
        inverse[pl.ds(off, PANEL), :] = band[:, n:]
        work[...] = work[...] - dot6(band[:, :n], band, ((0,), (0,)))
        return carry

    lax.fori_loop(first, last, panel, 0)


def orthonormal_kernel(
    mom_sq, grad_sq, basis_sq, mom_nw, grad_nw, basis_nw,
    buf_sq, buf_nw, left_out, back_sq, back_nw, squares_out,
    grad_sq_v, basis_sq_v, grad_nw_v, basis_nw_v,
    sq_hi, sq_lo, nw_hi, nw_lo,
    partial, held, projected, scatter_z,
    gram_part, gram_in, gram, chol_work, inverse,
    turned_hi, turned_lo,
    sums_0, sums_1, sums_2, sums_3, wide_0, wide_1, wide_2, wide_3,
    scatter_0, scatter_1, scatter_2, scatter_3, scatter_4, scatter_5, scatter_6, scatter_7,
    norms,
    load_sem, send_sem, recv_sem, gram_sem, norm_sem,
):
    f, t = lax.axis_index("fsdp"), lax.axis_index("tp")
    y, x = f // RING_X, lax.rem(f, RING_X)
    z, core = t // 2, lax.rem(t, 2)
    other = 1 - core
    fsdp_count = RING_X * RING_Y
    tp_count = RING_Z * 2
    links = Links(send_sem, recv_sem)
    gram_ruler = gram_in.at[pl.ds(0, fsdp_count - 1)]

    def at(y=y, x=x, z=z, core=core):
        return (y * RING_X + x, z * 2 + core)

    def step(value, by):
        return lax.rem(value + by, 4)

    sibling = at(core=other)
    x_ring = (x, at(x=step(x, 1)), at(x=step(x, 3)))
    y_ring = (y, at(y=step(y, 1)), at(y=step(y, 3)))
    z_ring = (z, at(z=step(z, 1)), at(z=step(z, 3)))

    barrier = pltpu.get_barrier_semaphore()

    def greet_fsdp(k, carry):
        peer = lax.rem(f + k, fsdp_count)
        pl.semaphore_signal(barrier, inc=1, device_id=(peer, t), device_id_type=MESH)
        return carry

    def greet_tp(k, carry):
        peer = lax.rem(t + k, tp_count)
        pl.semaphore_signal(barrier, inc=1, device_id=(f, peer), device_id_type=MESH)
        return carry

    loads = []

    def load(src, dst):
        c = pltpu.make_async_copy(src, dst, load_sem.at[len(loads)])
        c.start()
        loads.append(c)

    load(basis_nw, basis_nw_v)
    load(mom_nw, buf_nw)
    load(grad_nw, grad_nw_v)
    for k in range(2):
        load(basis_sq.at[k], basis_sq_v.at[k])
        load(mom_sq.at[k], buf_sq.at[k])
        load(grad_sq.at[k], grad_sq_v.at[k])
    lax.fori_loop(1, fsdp_count, greet_fsdp, 0)
    lax.fori_loop(1, tp_count, greet_tp, 0)

    def rows_of(which):
        return pl.ds(pl.multiple_of(which * 256, 256), 256)

    core_group = links.group(held)
    core_copies = [
        core_group.copy(partial.at[i, rows_of(other)], held.at[i], sibling) for i in range(4)
    ]

    def project(i, buf, grad, basis, hi, lo, greeted=True):
        pair = split(basis[...])
        for place, which in enumerate((other, core)):
            rows = rows_of(which)
            b = buf[rows, :] + grad[rows, :].astype(F32)
            buf[rows, :] = b
            b_hi, b_lo = split(b)
            hi[rows, :] = b_hi
            lo[rows, :] = b_lo
            partial[i, rows, :] = dot3((b_hi, b_lo), pair)
            if place == 0:
                if not greeted:
                    pl.semaphore_wait(barrier, fsdp_count + tp_count - 2)
                core_copies[i].start()

    def own_rows(r, i, a, n):
        return projected.at[i, pl.ds(pl.multiple_of(core * 256 + r * 128 + a, 64), n)]

    def held_rows(r):
        return lambda i, a, n: held.at[i, pl.ds(r * 128 + a, n)]

    z_sum = [Scatter(links, *z_ring, held_rows(r), 64, scatter_z.at[r]) for r in range(2)]
    z_all = [
        Gather(links, *z_ring, lambda i, a, n, r=r: own_rows(r, i, a, n), 64, scatter_z.at[r])
        for r in range(2)
    ]
    across_groups = [links.group(partial.at[r]) for r in range(2)]

    def core_send(r, i):
        view = own_rows(r, i, 0, 128)
        return across_groups[r].copy(view, view, sibling)

    across = [[core_send(r, step(z, by)) for by in (0, 3, 1, 2)] for r in range(2)]

    def z_turn(r):
        z_sum[r].end(lambda a, n: own_rows(r, z, a, n))
        z_all[r].start()
        across[r][0].start()

    def z_middle(r):
        z_all[r].middle()
        across[r][1].start()
        across[r][2].start()

    def z_end(r):
        z_all[r].end()
        across[r][3].start()

    for c in loads[:3]:
        c.wait()
    for k in range(2):
        project(
            2 + k, buf_nw.at[k], grad_nw_v.at[k], basis_nw_v.at[k], nw_hi.at[k], nw_lo.at[k], k > 0
        )
    for k in range(2):
        for c in loads[3 + k * 3 : 6 + k * 3]:
            c.wait()
        project(k, buf_sq.at[k], grad_sq_v.at[k], basis_sq_v.at[k], sq_hi.at[k], sq_lo.at[k])
    for i in (2, 3, 0, 1):
        core_copies[i].wait_recv()
        held[i] = held[i] + partial[i, rows_of(core), :]
    for r in range(2):
        z_sum[r].start()
    for r in range(2):
        z_sum[r].middle()
    for r in range(2):
        z_turn(r)

    for r in range(2):
        across[r][0].wait_recv()
    gram_cols = pl.ds(pl.multiple_of(core * 128, 128), 128)
    gram_part[...] = dot6(projected[z, :, gram_cols], projected[z], ((0,), (0,)))

    def gram_rows(i):
        return pl.ds(pl.multiple_of(i * 8, 8), 8)

    def gram_copy(peer, slot):
        return pltpu.make_async_remote_copy(
            src_ref=gram_part.at[gram_rows(peer)],
            dst_ref=gram_in.at[slot],
            send_sem=gram_sem.at[0],
            recv_sem=gram_sem.at[1],
            device_id=(peer, t),
            device_id_type=MESH,
        )

    def full_rows(i):
        return pl.ds(pl.multiple_of(core * 128 + i * 8, 8), 8)

    def gram_copy2(peer):
        view = gram.at[full_rows(f)]
        return pltpu.make_async_remote_copy(
            src_ref=view,
            dst_ref=view,
            send_sem=gram_sem.at[2],
            recv_sem=gram_sem.at[3],
            device_id=(peer, t),
            device_id_type=MESH,
        )

    def gram_wait(which):
        ruler = gram_ruler
        pltpu.make_async_copy(ruler, ruler, gram_sem.at[which]).wait()

    def gram_out(k, carry):
        gram_copy(lax.rem(f + k, fsdp_count), f).start()
        return carry

    def gram_out2(k, carry):
        gram_copy2(lax.rem(f + k, fsdp_count)).start()
        return carry

    lax.fori_loop(1, fsdp_count, gram_out, 0)
    z_middle(0)
    z_middle(1)
    gram_wait(1)
    gram_in[f] = gram_part[gram_rows(f), :]
    gram[full_rows(f), :] = jnp.sum(gram_in[...], axis=0)
    lax.fori_loop(1, fsdp_count, gram_out2, 0)
    z_end(0)
    z_end(1)
    gram_wait(3)
    half_rows = gram.at[pl.ds(pl.multiple_of(core * 128, 128), 128)]
    gram_across_group = links.group(half_rows)
    gram_across = gram_across_group.copy(half_rows, half_rows, sibling)
    gram_across.start()

    sums = (sums_0, sums_1, sums_2, sums_3)
    wides = (wide_0, wide_1, wide_2, wide_3)
    inboxes = (scatter_0, scatter_1, scatter_2, scatter_3)
    inboxes_2 = (scatter_4, scatter_5, scatter_6, scatter_7)
    outer = (x_ring, y_ring, x_ring, y_ring)
    inner = (y_ring, x_ring, y_ring, x_ring)

    def thick(ref):
        return lambda i, a, n: ref.at[pl.ds(pl.multiple_of(i * 64 + a, 32), n)]

    def thin(ref, p):
        place = outer[p][0] * 64
        return lambda i, a, n: ref.at[pl.ds(pl.multiple_of(place + i * 16 + a, 8), n)]

    sum_1 = [Scatter(links, *outer[p], thick(sums[p]), 32, inboxes[p]) for p in range(4)]
    sum_2 = [Scatter(links, *inner[p], thin(sums[p], p), 8, inboxes_2[p]) for p in range(4)]
    all_1 = [Gather(links, *inner[p], thin(wides[p], p), 8, inboxes_2[p]) for p in range(4)]
    all_2 = [Gather(links, *outer[p], thick(wides[p]), 32, inboxes[p]) for p in range(4)]

    def sum_1_end(p):
        sum_1[p].end(lambda a, n: thick(sums[p])(outer[p][0], a, n))
        sum_2[p].start()

    def sum_2_end(p):
        sum_2[p].end(lambda a, n: thin(wides[p], p)(inner[p][0], a, n))
        all_1[p].start()

    def all_1_end(p):
        all_1[p].end()
        all_2[p].start()

    half_cols = sq_hi.shape[2] // 2

    def narrow_back(k):
        sums[k][:, half_cols:] = dot3(split(projected[2 + k].T), (nw_hi[k], nw_lo[k]))

    def square_back(k):
        turned_hi[...], turned_lo[...] = split(projected[k].T)
        for h in range(2):
            cols = slice(h * half_cols, (h + 1) * half_cols)
            part = dot3((turned_hi[...], turned_lo[...]), (sq_hi[k, :, cols], sq_lo[k, :, cols]))
            sums[2 * k + h][:, :half_cols] = part
            sum_1[2 * k + h].start()

    for r in range(2):
        for c in across[r][1:]:
            c.wait_recv()
    narrow_back(0)
    narrow_back(1)
    square_back(0)
    square_back(1)

    gram_across.wait_recv()
    own_inverse = inverse.at[z]
    cholesky_start(gram, chol_work)

    class Band:
        def __init__(self, first, rows):
            share = rows // 2

            def part(i, a, n):
                row = pl.multiple_of(first + core * share + a, 16)
                return inverse.at[i, pl.ds(row, n)]

            ruler = partial.at[0, pl.ds(0, 3 * share)]
            self.ring = Gather(links, *z_ring, part, share // 2, ruler)
            self.group = links.group(ruler)
            views = [part(step(z, by), 0, share) for by in (3, 1, 2)]
            self.across = [self.group.copy(v, v, sibling) for v in views]

        def start(self):
            self.ring.start()

        def middle(self):
            self.ring.middle()
            self.across[0].start()
            self.across[1].start()

        def end(self):
            self.ring.end()
            self.across[2].start()

        def wait(self):
            for c in self.across:
                c.wait_recv()

    bands = [Band(0, 192), Band(192, 64)]

    def panels(first, last):
        cholesky_panels(chol_work, own_inverse, first, last)

    panels(0, 2)
    for p in (0, 1, 2, 3):
        sum_1[p].middle()
    panels(2, 4)
    for p in (0, 1):
        sum_1_end(p)
    panels(4, 5)
    for p in (2, 3):
        sum_1_end(p)
    for p in (0, 1):
        sum_2[p].middle()
    panels(5, 6)
    for p in (0, 1):
        sum_2_end(p)
    for p in (2, 3):
        sum_2[p].middle()
    panels(6, 7)
    for p in (0, 1):
        all_1[p].middle()
    for p in (2, 3):
        sum_2_end(p)
    for p in (0, 1):
        all_1_end(p)
    panels(7, 8)
    bands[0].start()
    bands[1].start()
    for p in (2, 3):
        all_1[p].middle()
    for p in (2, 3):
        all_1_end(p)
    bands[0].middle()
    bands[1].middle()
    for p in (0, 1):
        all_2[p].middle()
    bands[0].end()
    bands[1].end()
    for p in (2, 3):
        all_2[p].middle()
    bands[0].wait()
    bands[1].wait()

    for i in range(4):
        left_out[i] = dot3(split(projected[i]), split(inverse[i]), ((1,), (1,)))

    norms[t] = jnp.zeros((8, RANK), F32)

    def back_factor(i, source, target):
        back = dot3(split(inverse[i]), split(source))
        target[...] = back
        square = jnp.sum(back * back, axis=1, keepdims=True)
        square = jnp.broadcast_to(square, (RANK, 128)).T
        norms[t, pl.ds(i, 1), :] = norms[t, pl.ds(i, 1), :] + square[:1]

    for p in range(4):
        all_2[p].end()
        k, h = p // 2, p % 2
        cols = slice(h * half_cols, (h + 1) * half_cols)
        back_factor(k, wides[p][:, :half_cols], back_sq.at[k, :, cols])
        if k == 0:
            back_factor(2 + h, wides[p][:, half_cols:], back_nw.at[h])

    def norm_copy(peer):
        return pltpu.make_async_remote_copy(
            src_ref=norms.at[t],
            dst_ref=norms.at[t],
            send_sem=norm_sem.at[0],
            recv_sem=norm_sem.at[1],
            device_id=(f, peer),
            device_id_type=MESH,
        )

    def norm_wait(which):
        ruler = norms.at[pl.ds(0, tp_count - 1)]
        pltpu.make_async_copy(ruler, ruler, norm_sem.at[which]).wait()

    def norm_out(k, carry):
        norm_copy(lax.rem(t + k, tp_count)).start()
        return carry

    lax.fori_loop(1, tp_count, norm_out, 0)

    for group in [core_group, gram_across_group] + across_groups:
        group.drain()
    for band in bands:
        band.ring.group.drain()
        band.group.drain()
    for ring in z_sum + z_all + sum_1 + sum_2 + all_1 + all_2:
        ring.group.drain()
    gram_wait(0)
    gram_wait(2)
    norm_wait(1)
    squares_out[...] = jnp.sum(norms[...], axis=0)
    norm_wait(0)


def orthonormal(*args):
    mom_sq, grad_sq, basis_sq, mom_nw, grad_nw, basis_nw = args
    rows = mom_sq.shape[1]
    wide, thin = mom_sq.shape[2], mom_nw.shape[2]
    widths = (wide // 2 + thin, wide // 2 + thin, wide // 2, wide // 2)
    vmem = pltpu.VMEM
    dma = pltpu.SemaphoreType.DMA
    whole = pl.BlockSpec(memory_space=pltpu.VMEM)
    return pl.pallas_call(
        orthonormal_kernel,
        out_shape=(
            pltpu.VMEM(mom_sq.shape, F32),
            pltpu.VMEM(mom_nw.shape, F32),
            pltpu.VMEM((4, rows, RANK), F32),
            pltpu.VMEM((2, RANK, wide), F32),
            pltpu.VMEM((2, RANK, thin), F32),
            pltpu.VMEM((8, RANK), F32),
        ),
        in_specs=[pl.BlockSpec(memory_space=pltpu.HBM)] * 6,
        out_specs=(whole,) * 6,
        scratch_shapes=[
            vmem(grad_sq.shape, BF16),
            vmem(basis_sq.shape, F32),
            vmem(grad_nw.shape, BF16),
            vmem(basis_nw.shape, F32),
            vmem(mom_sq.shape, BF16),
            vmem(mom_sq.shape, BF16),
            vmem(mom_nw.shape, BF16),
            vmem(mom_nw.shape, BF16),
            vmem((4, rows, RANK), F32),
            vmem((4, rows // 2, RANK), F32),
            vmem((4, rows, RANK), F32),
            vmem((2, 6, rows // 8, RANK), F32),
            vmem((128, RANK), F32),
            vmem((16, 8, RANK), F32),
            vmem((RANK, RANK), F32),
            vmem((RANK, 2 * RANK), F32),
            vmem((4, RANK, RANK), F32),
            vmem((RANK, rows), BF16),
            vmem((RANK, rows), BF16),
            *[vmem((RANK, w), F32) for w in widths],
            *[vmem((RANK, w), F32) for w in widths],
            *[vmem((6, 32, w), F32) for w in widths],
            *[vmem((6, 8, w), F32) for w in widths],
            vmem((8, 8, RANK), F32),
            dma((9,)),
            dma((28,)),
            dma((127,)),
            dma((4,)),
            dma((2,)),
        ],
        compiler_params=pltpu.CompilerParams(
            collective_id=0, has_side_effects=True, vmem_limit_bytes=VMEM_LIMIT
        ),
        cost_estimate=pl.CostEstimate(flops=6 * 10**9, bytes_accessed=9 * 2**20, transcendentals=0),
        name="orthonormal",
    )(*(pltpu.with_memory_space_constraint(a, pltpu.HBM) for a in args))


def finish_kernel(
    scale_sq, scale_nw,
    buf_sq, buf_nw, left, back_sq, back_nw, squares,
    mom_sq_out, basis_sq_out, upd_sq_out, mom_nw_out, basis_nw_out, upd_nw_out,
    mom_sq, basis_sq, upd_sq, mom_nw, basis_nw, upd_nw, store_sem,
):
    rows = buf_sq.shape[1]
    pieces = 2
    piece = rows // pieces
    stores = []

    def store(src, dst):
        c = pltpu.make_async_copy(src, dst, store_sem.at[len(stores)])
        c.start()
        stores.append(c)

    def part(mom, upd, buf, factor, pair, divisor, scale):
        mom[...] = buf - mm((factor * (1.0 - MOMENTUM)).astype(BF16), pair[0])
        upd[...] = (scale * dot3(split(factor / divisor), pair)).astype(BF16)

    for k in range(2):
        divisor_sq, divisor_nw = (
            jnp.sqrt(squares[i : i + 1, :]) + 1e-06 for i in (k, 2 + k)
        )
        basis_sq[k] = back_sq[k].T / divisor_sq
        store(basis_sq.at[k], basis_sq_out.at[k])
        pair = split(back_sq[k])
        for p in range(pieces):
            r = pl.ds(p * piece, piece)
            part(mom_sq.at[k, r], upd_sq.at[k, r], buf_sq[k, r, :], left[k, r, :], pair, divisor_sq, scale_sq)
            store(mom_sq.at[k, r], mom_sq_out.at[k, r])
            store(upd_sq.at[k, r], upd_sq_out.at[k, r])
        basis_nw[k] = back_nw[k].T / divisor_nw
        part(mom_nw.at[k], upd_nw.at[k], buf_nw[k], left[2 + k], split(back_nw[k]), divisor_nw, scale_nw)
        store(mom_nw.at[k], mom_nw_out.at[k])
        store(basis_nw.at[k], basis_nw_out.at[k])
        store(upd_nw.at[k], upd_nw_out.at[k])
    for c in stores:
        c.wait()


def finish(buf_sq, buf_nw, left, back_sq, back_nw, squares, scale_sq, scale_nw):
    pairs, rows, wide = buf_sq.shape
    thin = buf_nw.shape[2]
    outs = (
        jax.ShapeDtypeStruct(buf_sq.shape, F32),
        jax.ShapeDtypeStruct((pairs, wide, RANK), F32),
        jax.ShapeDtypeStruct(buf_sq.shape, BF16),
        jax.ShapeDtypeStruct(buf_nw.shape, F32),
        jax.ShapeDtypeStruct((pairs, thin, RANK), F32),
        jax.ShapeDtypeStruct(buf_nw.shape, BF16),
    )

    def kernel(*refs):
        finish_kernel(scale_sq, scale_nw, *refs)

    return pl.pallas_call(
        kernel,
        out_shape=outs,
        in_specs=[pl.BlockSpec(memory_space=pltpu.VMEM)] * 6,
        out_specs=(pl.BlockSpec(memory_space=pltpu.HBM),) * 6,
        scratch_shapes=[pltpu.VMEM(o.shape, o.dtype) for o in outs]
        + [pltpu.SemaphoreType.DMA((16,))],
        compiler_params=pltpu.CompilerParams(vmem_limit_bytes=VMEM_LIMIT),
        cost_estimate=pl.CostEstimate(flops=3 * 10**9, bytes_accessed=9 * 2**20, transcendentals=0),
        name="finish",
    )(buf_sq, buf_nw, left, back_sq, back_nw, squares)


def local(momentum_square, grad_square, basis_square, momentum_narrow, grad_narrow, basis_narrow):
    parts = orthonormal(
        momentum_square, grad_square, basis_square, momentum_narrow, grad_narrow, basis_narrow
    )
    total_rows = momentum_square.shape[1] * lax.axis_size("fsdp")
    tp_count = lax.axis_size("tp")
    scale_sq = math.sqrt(total_rows * momentum_square.shape[2] * tp_count / RANK)
    scale_nw = math.sqrt(total_rows * momentum_narrow.shape[2] * tp_count / RANK)
    return finish(*parts, scale_sq, scale_nw)


def solution(mesh):
    by_both = P(None, "fsdp", "tp")
    by_tp = P(None, "tp", None)
    return jax.shard_map(
        local,
        mesh=mesh,
        in_specs=(by_both, by_both, by_tp, by_both, by_both, by_tp),
        out_specs=(by_both, by_tp, by_both, by_both, by_tp, by_both),
        check_vma=False,
    )
```

time: 106 us -> 90.9 us (0.86)
  Pallas kernels: 105 us -> 90 us
    pallas_call x2, Pallas kernels: 105 us -> 90 us  [the longest x1 85.6 us: orthonormal(): pl.pallas_call(orthonormal_kernel, out_shape=(pltpu.VMEM(mom_sq.shape, F3...]
where the time goes in v2:
time: 90.9 us; the launch traced here: 90.8 us
  Pallas kernels  90 us (99%)
    pallas_call x1, Pallas kernels, orthonormal(): pl.pallas_call(orthonormal_kernel, out_shape=(pltpu.VMEM(mom_sq.shape, F3...  85.6 us
    pallas_call x1, Pallas kernels, finish(): pl.pallas_call(kernel, out_shape=outs, in_specs=[pl.BlockSpec(memory_spac...  4.44 us

profile of v2, /device:TPU:1, one launch (start us, length us, event | category | flops | bytes accessed | tf_op | source)
XLA Modules:
  0.0 90.8 jit_solution(5681643548258995725)
XLA Ops:
  0.6 85.6 %orthonormal.1 = (f32[2,512,1024]{2,1,0:T(8,128)S(1)}, f32[2,512,128]{2,1,0:T(8,128)S(1)}, f32[4,512,256]{2,1,0:T(8,128)S(1)}, f32[2,256,1024]{2,1,0:T(8,128)S(1...) custom-call(f32[2,512,1024]{2,1,0:T(8,128)} %mom_sq.1, bf16[2,512,1024]{2,1,0:T(8,128)(2,1)} %grad_sq.1, ...), custom_call_target="tpu_custom_call" | custom-call | flops 6000000000 | bytes 9437184 | tf_op jit(solution)/shard_map/orthonormal/pallas_call | solution.py:583
  86.2 4.4 %finish.1 = (f32[2,512,1024]{2,1,0:T(8,128)}, f32[2,1024,256]{2,1,0:T(8,128)}, bf16[2,512,1024]{2,1,0:T(8,128)(2,1)}, f32[2,512,128]{2,1,0:T(8,128)}, f32[2,128,...) custom-call(f32[2,512,1024]{2,1,0:T(8,128)S(1)} %get-tuple-element.12.refs_0_, f32[2,512,128]{2,1,0:T(8,128)S(1)} %get-tuple-element.13.refs_1_, ...), custom_call_target="tpu_custom_call" | custom-call | flops 3000000000 | bytes 9437184 | tf_op jit(solution)/shard_map/finish/pallas_call | solution.py:690

commit v3 on v2

--- a/solution.py
+++ b/solution.py
@@ -87,8 +87,12 @@
         self.l3 = outgoing(5, part(self.before, h, h), left)
 
     def start(self):
-        for c in (self.r1, self.l1, self.r2, self.l2):
-            c.start()
+        self.r1.start()
+        self.l1.start()
+
+    def start_rest(self):
+        self.r2.start()
+        self.l2.start()
 
     def middle(self):
         h = self.half
@@ -138,6 +142,44 @@
     def end(self):
         self.r2.wait_recv()
         self.l2.wait_recv()
+
+
+class DirectScatter:
+    def __init__(self, links, me, device_of, part, rows, inbox):
+        self.me, self.part, self.rows, self.inbox = me, part, rows, inbox
+        self.group = links.group(inbox)
+        self.copies = []
+        for by in (2, 1, 3):
+            peer = lax.rem(me + by, 4)
+            view = part(peer, 0, rows)
+            self.copies.append(self.group.copy(view, inbox.at[by - 1], device_of(peer)))
+
+    def start(self):
+        for c in self.copies:
+            c.start()
+
+    def end(self, target):
+        for c in self.copies:
+            c.wait_recv()
+        own = self.part(self.me, 0, self.rows)[...]
+        target(0, self.rows)[...] = (own + self.inbox[0]) + (self.inbox[1] + self.inbox[2])
+
+
+class DirectGather:
+    def __init__(self, links, me, device_of, part, rows, ruler):
+        self.group = links.group(ruler)
+        view = part(me, 0, rows)
+        self.copies = [
+            self.group.copy(view, view, device_of(lax.rem(me + by, 4))) for by in (2, 1, 3)
+        ]
+
+    def start(self):
+        for c in self.copies:
+            c.start()
+
+    def end(self):
+        for c in self.copies:
+            c.wait_recv()
 
 
 def factor_block(a):
@@ -199,7 +241,7 @@
     turned_hi, turned_lo,
     sums_0, sums_1, sums_2, sums_3, wide_0, wide_1, wide_2, wide_3,
     scatter_0, scatter_1, scatter_2, scatter_3, scatter_4, scatter_5, scatter_6, scatter_7,
-    norms,
+    norms, rulers,
     load_sem, send_sem, recv_sem, gram_sem, norm_sem,
 ):
     f, t = lax.axis_index("fsdp"), lax.axis_index("tp")
@@ -293,6 +335,10 @@
 
     across = [[core_send(r, step(z, by)) for by in (0, 3, 1, 2)] for r in range(2)]
 
+    def z_wait(r):
+        for c in across[r][1:]:
+            c.wait_recv()
+
     def z_turn(r):
         z_sum[r].end(lambda a, n: own_rows(r, z, a, n))
         z_all[r].start()
@@ -320,17 +366,14 @@
     for i in (2, 3, 0, 1):
         core_copies[i].wait_recv()
         held[i] = held[i] + partial[i, rows_of(core), :]
-    for r in range(2):
-        z_sum[r].start()
-    for r in range(2):
-        z_sum[r].middle()
-    for r in range(2):
-        z_turn(r)
-
-    for r in range(2):
-        across[r][0].wait_recv()
-    gram_cols = pl.ds(pl.multiple_of(core * 128, 128), 128)
-    gram_part[...] = dot6(projected[z, :, gram_cols], projected[z], ((0,), (0,)))
+    z_sum[0].start()
+    z_sum[0].start_rest()
+    z_sum[1].start()
+    z_sum[0].middle()
+    z_sum[1].start_rest()
+    z_sum[1].middle()
+    z_turn(0)
+    z_turn(1)
 
     def gram_rows(i):
         return pl.ds(pl.multiple_of(i * 8, 8), 8)
@@ -371,21 +414,6 @@
         gram_copy2(lax.rem(f + k, fsdp_count)).start()
         return carry
 
-    lax.fori_loop(1, fsdp_count, gram_out, 0)
-    z_middle(0)
-    z_middle(1)
-    gram_wait(1)
-    gram_in[f] = gram_part[gram_rows(f), :]
-    gram[full_rows(f), :] = jnp.sum(gram_in[...], axis=0)
-    lax.fori_loop(1, fsdp_count, gram_out2, 0)
-    z_end(0)
-    z_end(1)
-    gram_wait(3)
-    half_rows = gram.at[pl.ds(pl.multiple_of(core * 128, 128), 128)]
-    gram_across_group = links.group(half_rows)
-    gram_across = gram_across_group.copy(half_rows, half_rows, sibling)
-    gram_across.start()
-
     sums = (sums_0, sums_1, sums_2, sums_3)
     wides = (wide_0, wide_1, wide_2, wide_3)
     inboxes = (scatter_0, scatter_1, scatter_2, scatter_3)
@@ -398,11 +426,24 @@
 
     def thin(ref, p):
         place = outer[p][0] * 64
-        return lambda i, a, n: ref.at[pl.ds(pl.multiple_of(place + i * 16 + a, 8), n)]
+        return lambda i, a, n: ref.at[pl.ds(pl.multiple_of(place + i * 16 + a, 16), n)]
 
     sum_1 = [Scatter(links, *outer[p], thick(sums[p]), 32, inboxes[p]) for p in range(4)]
-    sum_2 = [Scatter(links, *inner[p], thin(sums[p], p), 8, inboxes_2[p]) for p in range(4)]
-    all_1 = [Gather(links, *inner[p], thin(wides[p], p), 8, inboxes_2[p]) for p in range(4)]
+    def on_x(i):
+        return at(x=i)
+
+    def on_y(i):
+        return at(y=i)
+
+    across_of = (on_y, on_x, on_y, on_x)
+    sum_2 = [
+        DirectScatter(links, inner[p][0], across_of[p], thin(sums[p], p), 16, inboxes_2[p])
+        for p in range(4)
+    ]
+    all_1 = [
+        DirectGather(links, inner[p][0], across_of[p], thin(wides[p], p), 16, inboxes_2[p])
+        for p in range(4)
+    ]
     all_2 = [Gather(links, *outer[p], thick(wides[p]), 32, inboxes[p]) for p in range(4)]
 
     def sum_1_end(p):
@@ -420,7 +461,8 @@
     half_cols = sq_hi.shape[2] // 2
 
     def narrow_back(k):
-        sums[k][:, half_cols:] = dot3(split(projected[2 + k].T), (nw_hi[k], nw_lo[k]))
+        factor = split(projected[2 + k].T)
+        sums[3 * k][:, half_cols:] = dot3(factor, (nw_hi[k], nw_lo[k]))
 
     def square_back(k):
         turned_hi[...], turned_lo[...] = split(projected[k].T)
@@ -429,16 +471,28 @@
             part = dot3((turned_hi[...], turned_lo[...]), (sq_hi[k, :, cols], sq_lo[k, :, cols]))
             sums[2 * k + h][:, :half_cols] = part
             sum_1[2 * k + h].start()
+            if k == 0:
+                sum_1[h].start_rest()
 
     for r in range(2):
-        for c in across[r][1:]:
-            c.wait_recv()
-    narrow_back(0)
-    narrow_back(1)
-    square_back(0)
-    square_back(1)
-
+        across[r][0].wait_recv()
+    gram_cols = pl.ds(pl.multiple_of(core * 128, 128), 128)
+    gram_part[...] = dot6(projected[z, :, gram_cols], projected[z], ((0,), (0,)))
+    lax.fori_loop(1, fsdp_count, gram_out, 0)
+    z_middle(0)
+    gram_wait(1)
+    gram_in[f] = gram_part[gram_rows(f), :]
+    gram[full_rows(f), :] = jnp.sum(gram_in[...], axis=0)
+    lax.fori_loop(1, fsdp_count, gram_out2, 0)
+    z_middle(1)
+    gram_wait(3)
+    half_rows = gram.at[pl.ds(pl.multiple_of(core * 128, 128), 128)]
+    gram_across_group = links.group(half_rows)
+    gram_across = gram_across_group.copy(half_rows, half_rows, sibling)
+    gram_across.start()
+    z_end(0)
     gram_across.wait_recv()
+
     own_inverse = inverse.at[z]
     cholesky_start(gram, chol_work)
 
@@ -450,7 +504,7 @@
                 row = pl.multiple_of(first + core * share + a, 16)
                 return inverse.at[i, pl.ds(row, n)]
 
-            ruler = partial.at[0, pl.ds(0, 3 * share)]
+            ruler = rulers.at[pl.ds(0, 3 * share)]
             self.ring = Gather(links, *z_ring, part, share // 2, ruler)
             self.group = links.group(ruler)
             views = [part(step(z, by), 0, share) for by in (3, 1, 2)]
@@ -477,38 +531,41 @@
     def panels(first, last):
         cholesky_panels(chol_work, own_inverse, first, last)
 
-    panels(0, 2)
-    for p in (0, 1, 2, 3):
+    panels(0, 1)
+    z_end(1)
+    z_wait(0)
+    z_wait(1)
+    narrow_back(0)
+    square_back(0)
+    narrow_back(1)
+    square_back(1)
+    panels(1, 3)
+    for p in (0, 1):
         sum_1[p].middle()
-    panels(2, 4)
+    for p in (2, 3):
+        sum_1[p].start_rest()
+    panels(3, 4)
+    for p in (2, 3):
+        sum_1[p].middle()
+    panels(4, 6)
     for p in (0, 1):
         sum_1_end(p)
-    panels(4, 5)
+    panels(6, 7)
     for p in (2, 3):
         sum_1_end(p)
     for p in (0, 1):
-        sum_2[p].middle()
-    panels(5, 6)
-    for p in (0, 1):
         sum_2_end(p)
-    for p in (2, 3):
-        sum_2[p].middle()
-    panels(6, 7)
-    for p in (0, 1):
-        all_1[p].middle()
+    panels(7, 8)
+    bands[0].start()
+    bands[1].start()
     for p in (2, 3):
         sum_2_end(p)
     for p in (0, 1):
         all_1_end(p)
-    panels(7, 8)
-    bands[0].start()
-    bands[1].start()
-    for p in (2, 3):
-        all_1[p].middle()
+    bands[0].middle()
+    bands[1].middle()
     for p in (2, 3):
         all_1_end(p)
-    bands[0].middle()
-    bands[1].middle()
     for p in (0, 1):
         all_2[p].middle()
     bands[0].end()
@@ -518,9 +575,6 @@
     bands[0].wait()
     bands[1].wait()
 
-    for i in range(4):
-        left_out[i] = dot3(split(projected[i]), split(inverse[i]), ((1,), (1,)))
-
     norms[t] = jnp.zeros((8, RANK), F32)
 
     def back_factor(i, source, target):
@@ -530,13 +584,23 @@
         square = jnp.broadcast_to(square, (RANK, 128)).T
         norms[t, pl.ds(i, 1), :] = norms[t, pl.ds(i, 1), :] + square[:1]
 
-    for p in range(4):
+    def back_factors(p):
         all_2[p].end()
         k, h = p // 2, p % 2
         cols = slice(h * half_cols, (h + 1) * half_cols)
         back_factor(k, wides[p][:, :half_cols], back_sq.at[k, :, cols])
-        if k == 0:
-            back_factor(2 + h, wides[p][:, half_cols:], back_nw.at[h])
+        if k == h:
+            back_factor(2 + k, wides[p][:, half_cols:], back_nw.at[k])
+
+    def left_factor(i):
+        left_out[i] = dot3(split(projected[i]), split(inverse[i]), ((1,), (1,)))
+
+    for i in range(4):
+        left_factor(i)
+    back_factors(0)
+    back_factors(1)
+    back_factors(2)
+    back_factors(3)
 
     def norm_copy(peer):
         return pltpu.make_async_remote_copy(
@@ -576,7 +640,7 @@
     mom_sq, grad_sq, basis_sq, mom_nw, grad_nw, basis_nw = args
     rows = mom_sq.shape[1]
     wide, thin = mom_sq.shape[2], mom_nw.shape[2]
-    widths = (wide // 2 + thin, wide // 2 + thin, wide // 2, wide // 2)
+    widths = (wide // 2 + thin, wide // 2, wide // 2, wide // 2 + thin)
     vmem = pltpu.VMEM
     dma = pltpu.SemaphoreType.DMA
     whole = pl.BlockSpec(memory_space=pltpu.VMEM)
@@ -615,11 +679,12 @@
             *[vmem((RANK, w), F32) for w in widths],
             *[vmem((RANK, w), F32) for w in widths],
             *[vmem((6, 32, w), F32) for w in widths],
-            *[vmem((6, 8, w), F32) for w in widths],
+            *[vmem((3, 16, w), F32) for w in widths],
             vmem((8, 8, RANK), F32),
+            vmem((288, RANK), F32),
             dma((9,)),
             dma((28,)),
-            dma((127,)),
+            dma((111,)),
             dma((4,)),
             dma((2,)),
         ],

time: 90.9 us -> 84.8 us (0.933)
  Pallas kernels: 90 us -> 83.9 us
    pallas_call x1, Pallas kernels: 85.6 us -> 79.5 us  [orthonormal(): pl.pallas_call(orthonormal_kernel, out_shape=(pltpu.VMEM(mom_sq.shape, F3...]
where the time goes in v3:
time: 84.8 us; the launch traced here: 84.7 us
  Pallas kernels  83.9 us (99%)
    pallas_call x1, Pallas kernels, orthonormal(): pl.pallas_call(orthonormal_kernel, out_shape=(pltpu.VMEM(mom_sq.shape, F3...  79.5 us
    pallas_call x1, Pallas kernels, finish(): pl.pallas_call(kernel, out_shape=outs, in_specs=[pl.BlockSpec(memory_spac...  4.44 us

profile of v3, /device:TPU:1, one launch (start us, length us, event | category | flops | bytes accessed | tf_op | source)
XLA Modules:
  0.0 84.7 jit_solution(12589960841677649609)
XLA Ops:
  0.6 79.5 %orthonormal.1 = (f32[2,512,1024]{2,1,0:T(8,128)S(1)}, f32[2,512,128]{2,1,0:T(8,128)S(1)}, f32[4,512,256]{2,1,0:T(8,128)S(1)}, f32[2,256,1024]{2,1,0:T(8,128)S(1...) custom-call(f32[2,512,1024]{2,1,0:T(8,128)} %mom_sq.1, bf16[2,512,1024]{2,1,0:T(8,128)(2,1)} %grad_sq.1, ...), custom_call_target="tpu_custom_call" | custom-call | flops 6000000000 | bytes 9437184 | tf_op jit(solution)/shard_map/orthonormal/pallas_call | solution.py:647
  80.1 4.4 %finish.1 = (f32[2,512,1024]{2,1,0:T(8,128)}, f32[2,1024,256]{2,1,0:T(8,128)}, bf16[2,512,1024]{2,1,0:T(8,128)(2,1)}, f32[2,512,128]{2,1,0:T(8,128)}, f32[2,128,...) custom-call(f32[2,512,1024]{2,1,0:T(8,128)S(1)} %get-tuple-element.12.refs_0_, f32[2,512,128]{2,1,0:T(8,128)S(1)} %get-tuple-element.13.refs_1_, ...), custom_call_target="tpu_custom_call" | custom-call | flops 3000000000 | bytes 9437184 | tf_op jit(solution)/shard_map/finish/pallas_call | solution.py:755

commit v4 on v3

--- a/solution.py
+++ b/solution.py
@@ -480,58 +480,12 @@
     gram_part[...] = dot6(projected[z, :, gram_cols], projected[z], ((0,), (0,)))
     lax.fori_loop(1, fsdp_count, gram_out, 0)
     z_middle(0)
+    z_middle(1)
     gram_wait(1)
     gram_in[f] = gram_part[gram_rows(f), :]
     gram[full_rows(f), :] = jnp.sum(gram_in[...], axis=0)
     lax.fori_loop(1, fsdp_count, gram_out2, 0)
-    z_middle(1)
-    gram_wait(3)
-    half_rows = gram.at[pl.ds(pl.multiple_of(core * 128, 128), 128)]
-    gram_across_group = links.group(half_rows)
-    gram_across = gram_across_group.copy(half_rows, half_rows, sibling)
-    gram_across.start()
     z_end(0)
-    gram_across.wait_recv()
-
-    own_inverse = inverse.at[z]
-    cholesky_start(gram, chol_work)
-
-    class Band:
-        def __init__(self, first, rows):
-            share = rows // 2
-
-            def part(i, a, n):
-                row = pl.multiple_of(first + core * share + a, 16)
-                return inverse.at[i, pl.ds(row, n)]
-
-            ruler = rulers.at[pl.ds(0, 3 * share)]
-            self.ring = Gather(links, *z_ring, part, share // 2, ruler)
-            self.group = links.group(ruler)
-            views = [part(step(z, by), 0, share) for by in (3, 1, 2)]
-            self.across = [self.group.copy(v, v, sibling) for v in views]
-
-        def start(self):
-            self.ring.start()
-
-        def middle(self):
-            self.ring.middle()
-            self.across[0].start()
-            self.across[1].start()
-
-        def end(self):
-            self.ring.end()
-            self.across[2].start()
-
-        def wait(self):
-            for c in self.across:
-                c.wait_recv()
-
-    bands = [Band(0, 192), Band(192, 64)]
-
-    def panels(first, last):
-        cholesky_panels(chol_work, own_inverse, first, last)
-
-    panels(0, 1)
     z_end(1)
     z_wait(0)
     z_wait(1)
@@ -539,27 +493,73 @@
     square_back(0)
     narrow_back(1)
     square_back(1)
-    panels(1, 3)
+    gram_wait(3)
+    half_rows = gram.at[pl.ds(pl.multiple_of(core * 128, 128), 128)]
+    gram_across_group = links.group(half_rows)
+    gram_across = gram_across_group.copy(half_rows, half_rows, sibling)
+    gram_across.start()
+    gram_across.wait_recv()
+
+    own_inverse = inverse.at[z]
+    cholesky_start(gram, chol_work)
+
+    class Band:
+        def __init__(self, first, rows):
+            share = rows // 2
+
+            def part(i, a, n):
+                row = pl.multiple_of(first + core * share + a, 16)
+                return inverse.at[i, pl.ds(row, n)]
+
+            ruler = rulers.at[pl.ds(0, 3 * share)]
+            self.ring = Gather(links, *z_ring, part, share // 2, ruler)
+            self.group = links.group(ruler)
+            views = [part(step(z, by), 0, share) for by in (3, 1, 2)]
+            self.across = [self.group.copy(v, v, sibling) for v in views]
+
+        def start(self):
+            self.ring.start()
+
+        def middle(self):
+            self.ring.middle()
+            self.across[0].start()
+            self.across[1].start()
+
+        def end(self):
+            self.ring.end()
+            self.across[2].start()
+
+        def wait(self):
+            for c in self.across:
+                c.wait_recv()
+
+    bands = [Band(0, 192), Band(192, 64)]
+
+    def panels(first, last):
+        cholesky_panels(chol_work, own_inverse, first, last)
+
+    panels(0, 2)
     for p in (0, 1):
         sum_1[p].middle()
     for p in (2, 3):
         sum_1[p].start_rest()
-    panels(3, 4)
+    panels(2, 3)
     for p in (2, 3):
         sum_1[p].middle()
-    panels(4, 6)
+    panels(3, 5)
     for p in (0, 1):
         sum_1_end(p)
-    panels(6, 7)
+    panels(5, 6)
     for p in (2, 3):
         sum_1_end(p)
     for p in (0, 1):
         sum_2_end(p)
+    panels(6, 7)
+    for p in (2, 3):
+        sum_2_end(p)
     panels(7, 8)
     bands[0].start()
     bands[1].start()
-    for p in (2, 3):
-        sum_2_end(p)
     for p in (0, 1):
         all_1_end(p)
     bands[0].middle()
@@ -621,6 +621,11 @@
         return carry
 
     lax.fori_loop(1, tp_count, norm_out, 0)
+
+    for k in range(2):
+        for buf, i, back in ((buf_sq, k, back_sq), (buf_nw, 2 + k, back_nw)):
+            factor = (left_out[i] * (1.0 - MOMENTUM)).astype(BF16)
+            buf[k] = buf[k] - mm(factor, back[k].astype(BF16))
 
     for group in [core_group, gram_across_group] + across_groups:
         group.drain()
@@ -698,11 +703,11 @@
 
 def finish_kernel(
     scale_sq, scale_nw,
-    buf_sq, buf_nw, left, back_sq, back_nw, squares,
+    mom_sq, mom_nw, left, back_sq, back_nw, squares,
     mom_sq_out, basis_sq_out, upd_sq_out, mom_nw_out, basis_nw_out, upd_nw_out,
-    mom_sq, basis_sq, upd_sq, mom_nw, basis_nw, upd_nw, store_sem,
+    basis_sq, upd_sq, basis_nw, upd_nw, store_sem,
 ):
-    rows = buf_sq.shape[1]
+    rows = upd_sq.shape[1]
     pieces = 2
     piece = rows // pieces
     stores = []
@@ -712,10 +717,8 @@
         c.start()
         stores.append(c)
 
-    def part(mom, upd, buf, factor, pair, divisor, scale):
-        mom[...] = buf - mm((factor * (1.0 - MOMENTUM)).astype(BF16), pair[0])
-        upd[...] = (scale * dot3(split(factor / divisor), pair)).astype(BF16)
-
+    store(mom_sq, mom_sq_out)
+    store(mom_nw, mom_nw_out)
     for k in range(2):
         divisor_sq, divisor_nw = (
             jnp.sqrt(squares[i : i + 1, :]) + 1e-06 for i in (k, 2 + k)
@@ -725,28 +728,28 @@
         pair = split(back_sq[k])
         for p in range(pieces):
             r = pl.ds(p * piece, piece)
-            part(mom_sq.at[k, r], upd_sq.at[k, r], buf_sq[k, r, :], left[k, r, :], pair, divisor_sq, scale_sq)
-            store(mom_sq.at[k, r], mom_sq_out.at[k, r])
+            factor = split(left[k, r, :] / divisor_sq)
+            upd_sq[k, r, :] = (scale_sq * dot3(factor, pair)).astype(BF16)
             store(upd_sq.at[k, r], upd_sq_out.at[k, r])
         basis_nw[k] = back_nw[k].T / divisor_nw
-        part(mom_nw.at[k], upd_nw.at[k], buf_nw[k], left[2 + k], split(back_nw[k]), divisor_nw, scale_nw)
-        store(mom_nw.at[k], mom_nw_out.at[k])
         store(basis_nw.at[k], basis_nw_out.at[k])
+        factor = split(left[2 + k] / divisor_nw)
+        upd_nw[k] = (scale_nw * dot3(factor, split(back_nw[k]))).astype(BF16)
         store(upd_nw.at[k], upd_nw_out.at[k])
     for c in stores:
         c.wait()
 
 
-def finish(buf_sq, buf_nw, left, back_sq, back_nw, squares, scale_sq, scale_nw):
-    pairs, rows, wide = buf_sq.shape
-    thin = buf_nw.shape[2]
+def finish(mom_sq, mom_nw, left, back_sq, back_nw, squares, scale_sq, scale_nw):
+    pairs, rows, wide = mom_sq.shape
+    thin = mom_nw.shape[2]
     outs = (
-        jax.ShapeDtypeStruct(buf_sq.shape, F32),
+        jax.ShapeDtypeStruct(mom_sq.shape, F32),
         jax.ShapeDtypeStruct((pairs, wide, RANK), F32),
-        jax.ShapeDtypeStruct(buf_sq.shape, BF16),
-        jax.ShapeDtypeStruct(buf_nw.shape, F32),
+        jax.ShapeDtypeStruct(mom_sq.shape, BF16),
+        jax.ShapeDtypeStruct(mom_nw.shape, F32),
         jax.ShapeDtypeStruct((pairs, thin, RANK), F32),
-        jax.ShapeDtypeStruct(buf_nw.shape, BF16),
+        jax.ShapeDtypeStruct(mom_nw.shape, BF16),
     )
 
     def kernel(*refs):
@@ -757,12 +760,12 @@
         out_shape=outs,
         in_specs=[pl.BlockSpec(memory_space=pltpu.VMEM)] * 6,
         out_specs=(pl.BlockSpec(memory_space=pltpu.HBM),) * 6,
-        scratch_shapes=[pltpu.VMEM(o.shape, o.dtype) for o in outs]
-        + [pltpu.SemaphoreType.DMA((16,))],
+        scratch_shapes=[pltpu.VMEM(outs[i].shape, outs[i].dtype) for i in (1, 2, 4, 5)]
+        + [pltpu.SemaphoreType.DMA((12,))],
         compiler_params=pltpu.CompilerParams(vmem_limit_bytes=VMEM_LIMIT),
-        cost_estimate=pl.CostEstimate(flops=3 * 10**9, bytes_accessed=9 * 2**20, transcendentals=0),
+        cost_estimate=pl.CostEstimate(flops=2 * 10**9, bytes_accessed=9 * 2**20, transcendentals=0),
         name="finish",
-    )(buf_sq, buf_nw, left, back_sq, back_nw, squares)
+    )(mom_sq, mom_nw, left, back_sq, back_nw, squares)
 
 
 def local(momentum_square, grad_square, basis_square, momentum_narrow, grad_narrow, basis_narrow):

time: 84.8 us -> 81.7 us (0.963)
  Pallas kernels: 83.9 us -> 80.8 us
    pallas_call x1, Pallas kernels: 79.5 us -> 77.1 us  [orthonormal(): pl.pallas_call(orthonormal_kernel, out_shape=(pltpu.VMEM(mom_sq.shape, F3...]
where the time goes in v4:
time: 81.7 us; the launch traced here: 81.6 us
  Pallas kernels  80.8 us (99%)
    pallas_call x1, Pallas kernels, orthonormal(): pl.pallas_call(orthonormal_kernel, out_shape=(pltpu.VMEM(mom_sq.shape, F3...  77.1 us
    pallas_call x1, Pallas kernels, finish(): pl.pallas_call(kernel, out_shape=outs, in_specs=[pl.BlockSpec(memory_spac...  3.68 us

profile of v4, /device:TPU:1, one launch (start us, length us, event | category | flops | bytes accessed | tf_op | source)
XLA Modules:
  0.0 81.6 jit_solution(17430921073077628580)
XLA Ops:
  0.6 77.1 %orthonormal.1 = (f32[2,512,1024]{2,1,0:T(8,128)S(1)}, f32[2,512,128]{2,1,0:T(8,128)S(1)}, f32[4,512,256]{2,1,0:T(8,128)S(1)}, f32[2,256,1024]{2,1,0:T(8,128)S(1...) custom-call(f32[2,512,1024]{2,1,0:T(8,128)} %mom_sq.1, bf16[2,512,1024]{2,1,0:T(8,128)(2,1)} %grad_sq.1, ...), custom_call_target="tpu_custom_call" | custom-call | flops 6000000000 | bytes 9437184 | tf_op jit(solution)/shard_map/orthonormal/pallas_call | solution.py:652
  77.8 3.7 %finish.1 = (f32[2,512,1024]{2,1,0:T(8,128)}, f32[2,1024,256]{2,1,0:T(8,128)}, bf16[2,512,1024]{2,1,0:T(8,128)(2,1)}, f32[2,512,128]{2,1,0:T(8,128)}, f32[2,128,...) custom-call(f32[2,512,1024]{2,1,0:T(8,128)S(1)} %get-tuple-element.12.refs_0_, f32[2,512,128]{2,1,0:T(8,128)S(1)} %get-tuple-element.13.refs_1_, ...), custom_call_target="tpu_custom_call" | custom-call | flops 2000000000 | bytes 9437184 | tf_op jit(solution)/shard_map/finish/pallas_call | solution.py:758

commit v5 on v4

--- a/solution.py
+++ b/solution.py
@@ -550,6 +550,7 @@
     for p in (0, 1):
         sum_1_end(p)
     panels(5, 6)
+    bands[0].start()
     for p in (2, 3):
         sum_1_end(p)
     for p in (0, 1):
@@ -558,20 +559,19 @@
     for p in (2, 3):
         sum_2_end(p)
     panels(7, 8)
-    bands[0].start()
     bands[1].start()
     for p in (0, 1):
         all_1_end(p)
+    for p in (2, 3):
+        all_1_end(p)
     bands[0].middle()
     bands[1].middle()
+    for p in (0, 1):
+        all_2[p].middle()
     for p in (2, 3):
-        all_1_end(p)
-    for p in (0, 1):
         all_2[p].middle()
     bands[0].end()
     bands[1].end()
-    for p in (2, 3):
-        all_2[p].middle()
     bands[0].wait()
     bands[1].wait()
 

time: 81.7 us -> 81.1 us (level)
  no operation moved by 1% of the time
where the time goes in v5:
time: 81.1 us; the launch traced here: 81 us
  Pallas kernels  80.2 us (99%)
    pallas_call x1, Pallas kernels, orthonormal(): pl.pallas_call(orthonormal_kernel, out_shape=(pltpu.VMEM(mom_sq.shape, F3...  76.5 us
    pallas_call x1, Pallas kernels, finish(): pl.pallas_call(kernel, out_shape=outs, in_specs=[pl.BlockSpec(memory_spac...  3.68 us

profile of v5, /device:TPU:1, one launch (start us, length us, event | category | flops | bytes accessed | tf_op | source)
XLA Modules:
  0.0 81.0 jit_solution(1426873386193825897)
XLA Ops:
  0.6 76.5 %orthonormal.1 = (f32[2,512,1024]{2,1,0:T(8,128)S(1)}, f32[2,512,128]{2,1,0:T(8,128)S(1)}, f32[4,512,256]{2,1,0:T(8,128)S(1)}, f32[2,256,1024]{2,1,0:T(8,128)S(1...) custom-call(f32[2,512,1024]{2,1,0:T(8,128)} %mom_sq.1, bf16[2,512,1024]{2,1,0:T(8,128)(2,1)} %grad_sq.1, ...), custom_call_target="tpu_custom_call" | custom-call | flops 6000000000 | bytes 9437184 | tf_op jit(solution)/shard_map/orthonormal/pallas_call | solution.py:652
  77.2 3.7 %finish.1 = (f32[2,512,1024]{2,1,0:T(8,128)}, f32[2,1024,256]{2,1,0:T(8,128)}, bf16[2,512,1024]{2,1,0:T(8,128)(2,1)}, f32[2,512,128]{2,1,0:T(8,128)}, f32[2,128,...) custom-call(f32[2,512,1024]{2,1,0:T(8,128)S(1)} %get-tuple-element.12.refs_0_, f32[2,512,128]{2,1,0:T(8,128)S(1)} %get-tuple-element.13.refs_1_, ...), custom_call_target="tpu_custom_call" | custom-call | flops 2000000000 | bytes 9437184 | tf_op jit(solution)/shard_map/finish/pallas_call | solution.py:758
